TPU v7x, 32 devices: a whole 2x2x4 slice. The times are simulated.
32 devices in a mesh: groups: 2 (over x), span: 16 (over z, y, core).
Axes of the slice: x: 2, y: 2, z: 4, core: 2. Of those that a mesh axis runs over, the one named last changes fastest.
Arguments:
- queries: bfloat16 [8192, 1024], P(('groups', 'span')), parts along dimension 0, may hold values from -96 to 96
- keys: bfloat16 [8192, 1024], P(('groups', 'span')), parts along dimension 0, may hold values from -9 to 9
- values: bfloat16 [8192, 1024], P(('groups', 'span')), parts along dimension 0, may hold values from -6 to 6
- track: int32 [64, 16], P(('groups', 'span')), parts along dimension 0, may hold values 0 or 1
- out_weight: bfloat16 [1024, 1024], replicated, may hold values from -0.1875 to 0.1875
- grad_out: bfloat16 [8192, 1024], P(('groups', 'span')), parts along dimension 0, may hold values from -6 to 6
Outputs:
- query_grad: bfloat16 [8192, 1024], P(('groups', 'span')), parts along dimension 0
- key_grad: bfloat16 [8192, 1024], P(('groups', 'span')), parts along dimension 0
- value_grad: bfloat16 [8192, 1024], P(('groups', 'span')), parts along dimension 0
- weight_grad: float32 [2048, 1024], P(('groups', 'span')), parts along dimension 0
There are 2 independent parts, one for each index of `groups`. A program takes and returns all parts, laid end to end along the dimension named above; an argument that names none is the same for every part. Nothing has to cross between parts.
All inputs are finite; a program needn't handle non-finite values. No bound on the sum of `track` on one device may be relied on, other than what follows from the above.
Results may differ from a plain program's by a relative error of at most 0.039.
Values may be sent and summed in bfloat16 or wider, within the bound.
No kernel may reach another device: no remote copies, remote signals or barrier semaphores. Data moves between devices by JAX's collectives and lax.ppermute only.
A program may use at most 64 MiB of HBM per device.

v0:
```python
import jax
import jax.numpy as jnp
from jax import lax
from jax.sharding import PartitionSpec as P

HEADS = 16
BLOCK = 128
WINDOW = 8


def shifted(value, axis, steps):
    count = lax.axis_size(axis)
    initial, last = (max(0, -steps), min(count, count - steps))
    return lax.ppermute(value, axis, [(source, source + steps) for source in range(initial, last)])


def pair_grads(query_p, key_p, value_p, grad_p, allowed, local_count, scale):
    scores = jnp.einsum("rhd,khd->hrk", query_p, key_p, preferred_element_type=jnp.float32) * scale
    scores = jnp.where(allowed[None], scores, jnp.float32(-1e30))
    top = jnp.max(scores, axis=-1, keepdims=True)
    expo = jnp.exp(scores - top)
    probs = expo / jnp.sum(expo, axis=-1, keepdims=True)
    probs_low = probs.astype(jnp.bfloat16)
    attn = jnp.einsum(
        "hrk,khd->rhd", probs_low, value_p, preferred_element_type=jnp.float32
    ).astype(jnp.bfloat16)
    delta = jnp.einsum("rhd,rhd->hr", grad_p, attn, preferred_element_type=jnp.float32)
    dprob = jnp.einsum("rhd,khd->hrk", grad_p, value_p, preferred_element_type=jnp.float32)
    dscore = (probs * (dprob - delta[..., None])).astype(jnp.bfloat16)
    query_g = (
        jnp.einsum("hrk,khd->rhd", dscore, key_p, preferred_element_type=jnp.float32) * scale
    ).astype(jnp.bfloat16)
    key_g = (
        jnp.einsum(
            "hrk,rhd->khd", dscore[:, :, :local_count], query_p, preferred_element_type=jnp.float32
        )
        * scale
    ).astype(jnp.bfloat16)
    value_g = jnp.einsum(
        "hrk,rhd->khd", probs_low[:, :, :local_count], grad_p, preferred_element_type=jnp.float32
    ).astype(jnp.bfloat16)
    return (attn, query_g, key_g, value_g)


def shards(queries, keys, values, track, out_weight, grad_out):
    rows, width = queries.shape
    head_dim = width // HEADS
    pair_width = 2 * head_dim
    scale = head_dim ** (-0.5)
    span_id = lax.axis_index("span")
    stacked = jnp.stack([keys, values])
    received = [shifted(stacked, "span", distance) for distance in range(1, WINDOW + 1)]
    memory = jnp.concatenate(received, axis=1)
    all_keys = jnp.concatenate([keys, memory[0]], axis=0)
    all_values = jnp.concatenate([values, memory[1]], axis=0)
    grad_attn = lax.dot_general(
        grad_out, out_weight, (((1,), (1,)), ((), ())), preferred_element_type=jnp.float32
    ).astype(jnp.bfloat16)
    per_block = rows // BLOCK
    lookback = jnp.arange(WINDOW * per_block, dtype=jnp.int32) // per_block + 1
    block_ok = (track == 1) & (lookback[None, :] <= span_id)
    mem_ok = jnp.repeat(jnp.repeat(block_ok, BLOCK, axis=0), BLOCK, axis=1)
    position = jnp.arange(rows, dtype=jnp.int32)
    local_ok = position[:, None] >= position[None, :]
    allowed = jnp.concatenate([local_ok, mem_ok], axis=1)
    key_total = all_keys.shape[0]

    def head_pair(index, carry):
        attn_buf, query_buf, key_buf, value_buf = carry
        start = index * pair_width
        query_p = lax.dynamic_slice_in_dim(queries, start, pair_width, 1).reshape(rows, 2, head_dim)
        key_p = lax.dynamic_slice_in_dim(all_keys, start, pair_width, 1).reshape(
            key_total, 2, head_dim
        )
        value_p = lax.dynamic_slice_in_dim(all_values, start, pair_width, 1).reshape(
            key_total, 2, head_dim
        )
        grad_p = lax.dynamic_slice_in_dim(grad_attn, start, pair_width, 1).reshape(
            rows, 2, head_dim
        )
        attn, query_g, key_g, value_g = pair_grads(
            query_p, key_p, value_p, grad_p, allowed, rows, scale
        )
        attn_buf = lax.dynamic_update_slice_in_dim(
            attn_buf, attn.reshape(rows, pair_width), start, 1
        )
        query_buf = lax.dynamic_update_slice_in_dim(
            query_buf, query_g.reshape(rows, pair_width), start, 1
        )
        key_buf = lax.dynamic_update_slice_in_dim(
            key_buf, key_g.reshape(rows, pair_width), start, 1
        )
        value_buf = lax.dynamic_update_slice_in_dim(
            value_buf, value_g.reshape(rows, pair_width), start, 1
        )
        return (attn_buf, query_buf, key_buf, value_buf)

    empty = jnp.zeros((rows, width), jnp.bfloat16)
    attn_out, query_grad, key_grad, value_grad = lax.fori_loop(
        0, HEADS // 2, head_pair, (empty, empty, empty, empty)
    )
    weight_grad = lax.psum_scatter(
        lax.dot_general(
            attn_out, grad_out, (((0,), (0,)), ((), ())), preferred_element_type=jnp.float32
        ),
        "span",
        scatter_dimension=0,
        tiled=True,
    )
    return (query_grad, key_grad, value_grad, weight_grad)


def solution(mesh):
    in_specs = (
        P(("groups", "span"), None),
        P(("groups", "span"), None),
        P(("groups", "span"), None),
        P(("groups", "span"), None),
        P(),
        P(("groups", "span"), None),
    )
    out_specs = (
        P(("groups", "span"), None),
        P(("groups", "span"), None),
        P(("groups", "span"), None),
        P(("groups", "span"), None),
    )
    return jax.shard_map(shards, mesh=mesh, in_specs=in_specs, out_specs=out_specs, check_vma=False)
```

profile of v0, /device:TPU:11, one launch (start us, length us, event | category | flops | bytes accessed | tf_op | source)
XLA Modules:
  0.0 514.1 jit_solution(15153567718506939762)
XLA Ops:
  7.2 1.4 copy.12
  8.6 1.2 copy.10
  10.9 3.7 collective-permute-start
  14.6 3.1 collective-permute-start.1
  17.8 2.3 collective-permute-start.2
  20.0 3.2 collective-permute-start.3
  23.3 2.8 collective-permute-start.4
  26.8 1.3 broadcast_in_dim.50
  28.5 6.9 %collective-permute-done = bf16[2,256,1024]{1,2,0:T(8,128)(2,1)} collective-permute-done((bf16[2,256,1024]{1,2,0:T(8,128)(2,1)}, bf16[2,256,1024]{1,2,0:T(8,128)(2,1)}, u32[]{:S(2)}, u32[]{:S(2)}) %collective-permute-start) | collective-permute-done | bytes 1048608 | tf_op jit(solution)/shard_map/ppermute | solution.py:14
  35.3 5.1 %collective-permute-start.5 = (bf16[2,256,1024]{1,2,0:T(8,128)(2,1)}, bf16[2,256,1024]{1,2,0:T(8,128)(2,1)}, u32[]{:S(2)}, u32[]{:S(2)}) collective-permute-start(bf16[2,256,1024]{1,2,0:T(8,128)(2,1)} %pad_maximum_fusion.2), channel_id=1, source_target_pairs={{0,6},{1,7},{2,8},{3,9},{4,10},{5,11},{6,12},{7,13},{8,14},{9,15},... | collective-permute-start | bytes 3145736 | tf_op jit(solution)/shard_map/ppermute | solution.py:14
  41.3 18.0 %collective-permute-done.1 = bf16[2,256,1024]{1,2,0:T(8,128)(2,1)} collective-permute-done((bf16[2,256,1024]{1,2,0:T(8,128)(2,1)}, bf16[2,256,1024]{1,2,0:T(8,128)(2,1)}, u32[]{:S(2)}, u32[]{:S(2)}) %collective-permute-start.1) | collective-permute-done | bytes 1048608 | tf_op jit(solution)/shard_map/ppermute | solution.py:14
  59.4 2.3 collective-permute-start.6
  61.7 2.8 collective-permute-done.2
  64.5 5.2 %collective-permute-start.7 = (bf16[2,256,1024]{1,2,0:T(8,128)(2,1)}, bf16[2,256,1024]{1,2,0:T(8,128)(2,1)}, u32[]{:S(2)}, u32[]{:S(2)}) collective-permute-start(bf16[2,256,1024]{1,2,0:T(8,128)(2,1)} %pad_maximum_fusion.2), channel_id=1, source_target_pairs={{0,8},{1,9},{2,10},{3,11},{4,12},{5,13},{6,14},{7,15},{16,24},{17,... | collective-permute-start | bytes 3145736 | tf_op jit(solution)/shard_map/ppermute | solution.py:14
  69.7 2.6 convolution_convert_fusion.2
  72.3 1.4 constant_dynamic-update-slice_fusion.11
  73.7 1.4 constant_dynamic-update-slice_fusion.10
  75.1 1.4 constant_dynamic-update-slice_fusion.9
  76.4 1.4 constant_dynamic-update-slice_fusion.8
  77.8 5.4 %collective-permute-done.4 = bf16[2,256,1024]{1,2,0:T(8,128)(2,1)} collective-permute-done((bf16[2,256,1024]{1,2,0:T(8,128)(2,1)}, bf16[2,256,1024]{1,2,0:T(8,128)(2,1)}, u32[]{:S(2)}, u32[]{:S(2)}) %collective-permute-start.4) | collective-permute-done | bytes 1048608 | tf_op jit(solution)/shard_map/ppermute | solution.py:14
  83.2 1.4 constant_dynamic-update-slice_fusion.7
  84.6 21.1 %collective-permute-done.5 = bf16[2,256,1024]{1,2,0:T(8,128)(2,1)} collective-permute-done((bf16[2,256,1024]{1,2,0:T(8,128)(2,1)}, bf16[2,256,1024]{1,2,0:T(8,128)(2,1)}, u32[]{:S(2)}, u32[]{:S(2)}) %collective-permute-start.5) | collective-permute-done | bytes 1048608 | tf_op jit(solution)/shard_map/ppermute | solution.py:14
  105.7 1.4 constant_dynamic-update-slice_fusion.6
  107.1 54.8 %collective-permute-done.6 = bf16[2,256,1024]{1,2,0:T(8,128)(2,1)} collective-permute-done((bf16[2,256,1024]{1,2,0:T(8,128)(2,1)}, bf16[2,256,1024]{1,2,0:T(8,128)(2,1)}, u32[]{:S(2)}, u32[]{:S(2)}) %collective-permute-start.6) | collective-permute-done | bytes 1048608 | tf_op jit(solution)/shard_map/ppermute | solution.py:14
  161.9 1.4 constant_dynamic-update-slice_fusion.5
  163.3 14.9 %collective-permute-done.7 = bf16[2,256,1024]{1,2,0:T(8,128)(2,1)} collective-permute-done((bf16[2,256,1024]{1,2,0:T(8,128)(2,1)}, bf16[2,256,1024]{1,2,0:T(8,128)(2,1)}, u32[]{:S(2)}, u32[]{:S(2)}) %collective-permute-start.7) | collective-permute-done | bytes 1048608 | tf_op jit(solution)/shard_map/ppermute | solution.py:14
  178.1 1.4 constant_dynamic-update-slice_fusion.4
  179.5 1.2 slice_bitcast_fusion
  180.7 4.0 pad_maximum_fusion
  188.1 159.1 %while.19 = (s32[]{:T(128)}, bf16[256,1024]{0,1:T(8,128)(2,1)}, bf16[256,1024]{1,0:T(8,128)(2,1)}, bf16[256,1024]{1,0:T(8,128)(2,1)}, bf16[256,1024]{1,0:T(8,128...) while((s32[]{:T(128)}, bf16[256,1024]{0,1:T(8,128)(2,1)}, ...), condition=%wide.region_3.4_spmd, body=%wide.region_0.3_spmd.sunk | while | flops 649660160 | bytes 69216552 | solution.py:99
  192.3 5.0 fusion.63
  197.3 3.0 fusion.64
  204.9 1.1 convolution_convert_fusion.4
  206.1 1.1 fusion.68
  212.2 5.0 fusion.63
  217.2 3.0 fusion.64
  224.8 1.1 convolution_convert_fusion.4
  226.0 1.1 fusion.68
  232.1 5.0 fusion.63
  237.1 3.0 fusion.64
  244.6 1.1 convolution_convert_fusion.4
  245.9 1.1 fusion.68
  251.9 5.0 fusion.63
  256.9 3.0 fusion.64
  264.5 1.1 convolution_convert_fusion.4
  265.8 1.1 fusion.68
  271.8 5.0 fusion.63
  276.8 3.0 fusion.64
  284.4 1.1 convolution_convert_fusion.4
  285.7 1.1 fusion.68
  291.7 5.0 fusion.63
  296.7 3.0 fusion.64
  304.3 1.1 convolution_convert_fusion.4
  305.5 1.1 fusion.68
  311.6 5.0 fusion.63
  316.6 3.0 fusion.64
  324.2 1.1 convolution_convert_fusion.4
  325.4 1.1 fusion.68
  331.5 5.0 fusion.63
  336.5 3.0 fusion.64
  344.1 1.1 convolution_convert_fusion.4
  345.3 1.1 fusion.68
  347.2 3.9 fusion.18
  351.1 156.1 %reduce-scatter.2.cloned.1.call-done = f32[64,1024]{1,0:T(8,128)} async-done(((f32[1024,1024]{1,0:T(8,128)}), f32[64,1024]{1,0:T(8,128)}) %reduce-scatter.2.cloned.1.call-update) | async-done | bytes 262160 | tf_op jit(solution)/shard_map/reduce_scatter | solution.py:102
  (184 shorter events, 83.0 us)
Async XLA Ops:
  7.2 62.6 %copy-start = (bf16[1024,1024]{1,0:T(8,128)(2,1)S(1)}, bf16[1024,1024]{1,0:T(8,128)(2,1)}, u32[]{:S(2)}) copy-start(bf16[1024,1024]{1,0:T(8,128)(2,1)} %param.12) | copy-start | bytes 6291460
  7.2 500.0 %reduce-scatter.2.cloned.1.call-start = ((), (), s32[]{:S(2)}) async-start(), calls=%async_computation.1 | async-start | bytes 4456448 | tf_op jit(solution)/shard_map/reduce_scatter | solution.py:102
  10.9 24.4 %collective-permute-start = (bf16[2,256,1024]{1,2,0:T(8,128)(2,1)}, bf16[2,256,1024]{1,2,0:T(8,128)(2,1)}, u32[]{:S(2)}, u32[]{:S(2)}) collective-permute-start(bf16[2,256,1024]{1,2,0:T(8,128)(2,1)} %pad_maximum_fusion.2), channel_id=1, source_target_pairs={{0,1},{1,2},{2,3},{3,4},{4,5},{5,6},{6,7},{7,8},{8,9},{9,10},{10,1... | collective-permute-start | bytes 3145736 | tf_op jit(solution)/shard_map/ppermute | solution.py:14
  14.6 44.7 %collective-permute-start.1 = (bf16[2,256,1024]{1,2,0:T(8,128)(2,1)}, bf16[2,256,1024]{1,2,0:T(8,128)(2,1)}, u32[]{:S(2)}, u32[]{:S(2)}) collective-permute-start(bf16[2,256,1024]{1,2,0:T(8,128)(2,1)} %pad_maximum_fusion.2), channel_id=1, source_target_pairs={{0,2},{1,3},{2,4},{3,5},{4,6},{5,7},{6,8},{7,9},{8,10},{9,11},{10,... | collective-permute-start | bytes 3145736 | tf_op jit(solution)/shard_map/ppermute | solution.py:14
  17.8 46.7 %collective-permute-start.2 = (bf16[2,256,1024]{1,2,0:T(8,128)(2,1)}, bf16[2,256,1024]{1,2,0:T(8,128)(2,1)}, u32[]{:S(2)}, u32[]{:S(2)}) collective-permute-start(bf16[2,256,1024]{1,2,0:T(8,128)(2,1)} %pad_maximum_fusion.2), channel_id=1, source_target_pairs={{0,3},{1,4},{2,5},{3,6},{4,7},{5,8},{6,9},{7,10},{8,11},{9,12},{10... | collective-permute-start | bytes 3145736 | tf_op jit(solution)/shard_map/ppermute | solution.py:14
  20.0 56.4 %collective-permute-start.3 = (bf16[2,256,1024]{1,2,0:T(8,128)(2,1)}, bf16[2,256,1024]{1,2,0:T(8,128)(2,1)}, u32[]{:S(2)}, u32[]{:S(2)}) collective-permute-start(bf16[2,256,1024]{1,2,0:T(8,128)(2,1)} %pad_maximum_fusion.2), channel_id=1, source_target_pairs={{0,4},{1,5},{2,6},{3,7},{4,8},{5,9},{6,10},{7,11},{8,12},{9,13},{1... | collective-permute-start | bytes 3145736 | tf_op jit(solution)/shard_map/ppermute | solution.py:14
  23.3 60.0 %collective-permute-start.4 = (bf16[2,256,1024]{1,2,0:T(8,128)(2,1)}, bf16[2,256,1024]{1,2,0:T(8,128)(2,1)}, u32[]{:S(2)}, u32[]{:S(2)}) collective-permute-start(bf16[2,256,1024]{1,2,0:T(8,128)(2,1)} %pad_maximum_fusion.2), channel_id=1, source_target_pairs={{0,5},{1,6},{2,7},{3,8},{4,9},{5,10},{6,11},{7,12},{8,13},{9,14},{... | collective-permute-start | bytes 3145736 | tf_op jit(solution)/shard_map/ppermute | solution.py:14
  35.3 70.4 %collective-permute-start.5 = (bf16[2,256,1024]{1,2,0:T(8,128)(2,1)}, bf16[2,256,1024]{1,2,0:T(8,128)(2,1)}, u32[]{:S(2)}, u32[]{:S(2)}) collective-permute-start(bf16[2,256,1024]{1,2,0:T(8,128)(2,1)} %pad_maximum_fusion.2), channel_id=1, source_target_pairs={{0,6},{1,7},{2,8},{3,9},{4,10},{5,11},{6,12},{7,13},{8,14},{9,15},... | collective-permute-start | bytes 3145736 | tf_op jit(solution)/shard_map/ppermute | solution.py:14
  59.4 102.5 %collective-permute-start.6 = (bf16[2,256,1024]{1,2,0:T(8,128)(2,1)}, bf16[2,256,1024]{1,2,0:T(8,128)(2,1)}, u32[]{:S(2)}, u32[]{:S(2)}) collective-permute-start(bf16[2,256,1024]{1,2,0:T(8,128)(2,1)} %pad_maximum_fusion.2), channel_id=1, source_target_pairs={{0,7},{1,8},{2,9},{3,10},{4,11},{5,12},{6,13},{7,14},{8,15},{16,23... | collective-permute-start | bytes 3145736 | tf_op jit(solution)/shard_map/ppermute | solution.py:14
  64.5 113.6 %collective-permute-start.7 = (bf16[2,256,1024]{1,2,0:T(8,128)(2,1)}, bf16[2,256,1024]{1,2,0:T(8,128)(2,1)}, u32[]{:S(2)}, u32[]{:S(2)}) collective-permute-start(bf16[2,256,1024]{1,2,0:T(8,128)(2,1)} %pad_maximum_fusion.2), channel_id=1, source_target_pairs={{0,8},{1,9},{2,10},{3,11},{4,12},{5,13},{6,14},{7,15},{16,24},{17,... | collective-permute-start | bytes 3145736 | tf_op jit(solution)/shard_map/ppermute | solution.py:14
  197.3 4.5 copy-start.2
  200.3 2.4 copy-start.1
  202.7 1.4 copy-start.3
  217.2 4.5 copy-start.2
  220.2 2.4 copy-start.1
  222.6 1.4 copy-start.3
  237.0 4.5 copy-start.2
  240.1 2.4 copy-start.1
  242.5 1.4 copy-start.3
  256.9 4.5 copy-start.2
  259.9 2.4 copy-start.1
  262.4 1.4 copy-start.3
  276.8 4.5 copy-start.2
  279.8 2.4 copy-start.1
  282.3 1.4 copy-start.3
  296.7 4.5 copy-start.2
  299.7 2.4 copy-start.1
  302.1 1.4 copy-start.3
  316.6 4.5 copy-start.2
  319.6 2.4 copy-start.1
  322.0 1.4 copy-start.3
  336.5 4.5 copy-start.2
  339.5 2.4 copy-start.1
  341.9 1.4 copy-start.3
Sparse Core Ops, SparseCore 0:
  351.2 155.9 reduce-scatter.1
where the time goes:
time: 521 us; the launch traced here: 514 us
  waiting for transfers between devices  280 us (54%)
  matrix products  85 us (16%)
  local copies, waits for them, and re-layouts  75.6 us (15%)
  other arithmetic  30.6 us (6%)
  starting transfers between devices  27.9 us (5%)
  between operations  14.2 us (3%)
    reduce_scatter x1, waiting for transfers between devices, shards(): lax.psum_scatter(lax.dot_general(attn_out, grad_out, (((0,), (0,)), ((),...  156 us
    ppermute x8, waiting for transfers between devices, shifted(): lax.ppermute(value, axis, [(source, source + steps) for source in range(i...  124 us
    sub x8, matrix products, pair_grads(): expo = jnp.exp(scores - top)  39.9 us
    ppermute x8, starting transfers between devices, shifted(): lax.ppermute(value, axis, [(source, source + steps) for source in range(i...  27.8 us
    convert_element_type x8, other arithmetic, pair_grads(): probs_low = probs.astype(jnp.bfloat16)  24 us
    unnamed x12, local copies, waits for them, and re-layouts  12.5 us
  transfers between devices with their start and end apart: 9, of which 8 were waited for; matrix products, arithmetic and copies ran while one was open for 3% of the time, Pallas kernels for 0%

commit v1 on v0

v1 whole, which is shorter than its diff:
```python
import functools

import jax
import jax.numpy as jnp
from jax import lax
from jax.experimental import pallas as pl
from jax.experimental.pallas import tpu as pltpu
from jax.sharding import PartitionSpec as P

HEADS = 16
BLOCK = 128
WINDOW = 8
ROW = 4
LANES = 128
NEG = -1e30
PAD = 3e30
VMEM_LIMIT = 48 * 1024 * 1024

F32 = jnp.float32
BF16 = jnp.bfloat16

ANY = pl.BlockSpec(memory_space=pl.ANY)
SMEM = pl.BlockSpec(memory_space=pltpu.SMEM)
VMEM = pl.BlockSpec(memory_space=pltpu.VMEM)


def nn(a, b):
    return lax.dot_general(a, b, (((1,), (0,)), ((), ())), preferred_element_type=F32)


def nt(a, b):
    return lax.dot_general(a, b, (((1,), (1,)), ((), ())), preferred_element_type=F32)


def params():
    return pltpu.CompilerParams(vmem_limit_bytes=VMEM_LIMIT)


def split_pair(a, b):
    lane = lax.broadcasted_iota(jnp.int32, a.shape, 1)
    low = lane < LANES // 2
    even = jnp.where(low, a, pltpu.roll(b, LANES // 2, 1))
    odd = jnp.where(low, pltpu.roll(a, LANES // 2, 1), b)
    return even, odd


def pack_kernel(me_ref, q_ref, k_ref, v_ref, t_ref, own_ref, *outs):
    first, second = outs[:ROW], outs[ROW:]
    r = me_ref[0]
    odd_me = (r % 2) == 1
    rows = q_ref.shape[0]
    per = rows // BLOCK

    def pieces(src, chunk, pair):
        tile = 4 * chunk + (r // 2 + pair) % 2
        a = src[:, pl.ds(pl.multiple_of(tile * LANES, LANES), LANES)].astype(F32)
        b = src[:, pl.ds(pl.multiple_of((tile + 2) * LANES, LANES), LANES)].astype(F32)
        even, odd = split_pair(a, b)
        return jnp.where(odd_me, odd, even), jnp.where(odd_me, even, odd)

    for chunk in (0, 1):
        for pair in (0, 1):
            for which, src in enumerate((k_ref, v_ref)):
                for side, value in enumerate(pieces(src, chunk, pair)):
                    value = value.astype(BF16)
                    d = 2 * pair + side
                    target = (first, second)[chunk][d]
                    target[which * rows : (which + 1) * rows, :] = value
                    if d == 0:
                        base = (2 * chunk + which) * rows
                        own_ref[base : base + rows, :] = value
            for side, value in enumerate(pieces(q_ref, chunk, pair)):
                d = 2 * pair + side
                scaled = value * 0.125
                for b in range(per):
                    base = 2 * rows + (chunk * per + b) * LANES
                    turned = scaled[b * BLOCK : (b + 1) * BLOCK].T
                    second[d][base : base + LANES, :] = turned.astype(BF16)
    for d in range(ROW):
        second[d][4 * rows : 4 * rows + 16, :] = t_ref[...]


def pack(me, queries, keys, values, track_block):
    rows = queries.shape[0]
    one = jax.ShapeDtypeStruct((2 * rows, LANES), BF16)
    two = jax.ShapeDtypeStruct((4 * rows + 16, LANES), BF16)
    own = jax.ShapeDtypeStruct((4 * rows, LANES), BF16)
    outs = pl.pallas_call(
        pack_kernel,
        out_shape=(own,) + (one,) * ROW + (two,) * ROW,
        in_specs=[SMEM] + [VMEM] * 4,
        out_specs=[VMEM] * 9,
        compiler_params=params(),
        name="pack",
    )(me, queries, keys, values, track_block)
    return outs[0], outs[1:5], outs[5:]


def plan_kernel(me_ref, track_ref, list_ref, count_ref):
    r = me_ref[0]
    z = me_ref[1]

    def one_query(qi, carry):
        d = qi // 2
        rho = r ^ d
        span = ROW * z + rho

        def clear(i, c):
            list_ref[qi, i] = 0
            return c

        lax.fori_loop(0, 24, clear, 0)

        def step(i, state):
            near, total = state
            u = span - (i // 2 + 1)
            use = jnp.logical_and(track_ref[qi, i] == 1, u >= 0)
            safe = jnp.maximum(u, 0)
            back = z - safe // ROW
            slot = ((back * ROW + (r ^ (safe % ROW))) * 4) + i % 2

            @pl.when(use)
            def _():
                list_ref[qi, total] = slot

            use = use.astype(jnp.int32)
            near = near + jnp.where(back < 2, use, 0)
            return near, total + use

        near, total = lax.fori_loop(0, 2 * WINDOW, step, (0, 0))
        count_ref[qi, 0] = near
        count_ref[qi, 1] = total
        return carry

    lax.fori_loop(0, 2 * ROW, one_query, 0)


def plan(me, track_row):
    return pl.pallas_call(
        plan_kernel,
        out_shape=(
            jax.ShapeDtypeStruct((2 * ROW, 24), jnp.int32),
            jax.ShapeDtypeStruct((2 * ROW, 2), jnp.int32),
        ),
        in_specs=[SMEM, SMEM],
        out_specs=[SMEM, SMEM],
        name="plan",
    )(me, track_row)


def block_diag(x):
    row = lax.broadcasted_iota(jnp.int32, x.shape, 0)
    zero = jnp.zeros_like(x)
    top = row < LANES // 2
    return jnp.concatenate([jnp.where(top, x, zero), jnp.where(top, zero, x)], axis=1)


def pick_heads(x):
    row = lax.broadcasted_iota(jnp.int32, (LANES, LANES), 0)
    return jnp.where(row < LANES // 2, x[:, :LANES], x[:, LANES:])


def causal(shape):
    key = lax.broadcasted_iota(jnp.int32, shape, 0)
    query = lax.broadcasted_iota(jnp.int32, shape, 1) % BLOCK
    return key <= query


def row_copies(chunk, rows, back, own, rest, kv, sem, slot):
    base = back * 4 * ROW
    out = []
    own_blocks = own.reshape(8, BLOCK, LANES)
    rest_blocks = rest.reshape(12, BLOCK, LANES)
    out.append(
        pltpu.make_async_copy(own_blocks.at[pl.ds(4 * chunk, 4)], kv.at[pl.ds(base, 4)], sem.at[slot])
    )
    out.append(pltpu.make_async_copy(rest_blocks, kv.at[pl.ds(base + 4, 12)], sem.at[slot + 1]))
    return out


def query_copies(chunk, seconds, qt, sem, slot):
    out = []
    for d, second in enumerate(seconds):
        blocks = second.at[pl.ds(512 + chunk * 256, 256)].reshape(2, BLOCK, LANES)
        out.append(pltpu.make_async_copy(blocks, qt.at[pl.ds(2 * d, 2)], sem.at[slot + d]))
    return out


def slots_of(list_ref, qi, start, count, how_many, base=0):
    fs, pads = [], []
    for i in range(how_many):
        position = start + i
        inside = position < count
        fs.append(jnp.where(inside, list_ref[qi, jnp.minimum(position, 23)] - base, 0))
        pads.append(jnp.where(inside, 0.0, PAD).astype(F32))
    return fs, pads


def fwd_group(kv, vt, q2, fs, pads, diag=None):
    keys = jnp.concatenate([kv[f] for f in fs], axis=0)
    scores = nn(keys, q2)
    parts = []
    top = None
    for i, pad in enumerate(pads):
        part = scores[i * BLOCK : (i + 1) * BLOCK]
        if diag == i:
            part = jnp.where(causal(part.shape), part, NEG)
        peak = jnp.maximum(jnp.max(part, axis=0, keepdims=True) - pad, NEG)
        top = peak if top is None else jnp.maximum(top, peak)
        parts.append(part)
    expo = [jnp.exp(part - (top + pad)).astype(BF16) for part, pad in zip(parts, pads)]
    turned = jnp.concatenate([vt[f] for f in fs], axis=1)
    return top, nn(turned, jnp.concatenate(expo, axis=0))


def merge(m_ref, acc_ref, qi, top, add):
    old = m_ref[qi, 0:1, :]
    new = jnp.maximum(old, top)
    acc_ref[qi] = acc_ref[qi] * jnp.exp(old - new) + add * jnp.exp(top - new)
    m_ref[qi] = jnp.broadcast_to(new, m_ref.shape[1:])


def turn_values(kv, vt, blocks, base):
    for f in blocks:
        vt[f - base, 0:LANES, :] = kv[f - base + 2].astype(F32).T.astype(BF16)
        vt[f - base, LANES : LANES + 16, :] = jnp.ones((16, LANES), BF16)


def near_kernel(
    chunk, list_ref, count_ref, own0, rest0, own1, rest1, s0, s1, s2, s3, m_ref, acc_ref, kv, vt, qt, sem
):
    copies = row_copies(chunk, 256, 0, own0, rest0, kv, sem, 0)
    copies += row_copies(chunk, 256, 1, own1, rest1, kv, sem, 2)
    copies += query_copies(chunk, (s0, s1, s2, s3), qt, sem, 4)
    for copy in copies:
        copy.start()
    for copy in copies:
        copy.wait()
    turn_values(kv, vt, [4 * i + b for i in range(2 * ROW) for b in (0, 1)], 0)
    for d in range(ROW):
        q2 = [block_diag(qt[2 * d + b]) for b in (0, 1)]
        counts = [count_ref[2 * d + b, 0] for b in (0, 1)]
        for b in (0, 1):
            qi = 2 * d + b
            fs, pads = slots_of(list_ref, qi, 0, counts[b], 2)
            fs = [4 * d, 4 * d + b] + fs
            pads = [jnp.float32(0.0 if b else PAD), jnp.float32(0.0)] + pads
            top, add = fwd_group(kv, vt, q2[b], fs, pads, diag=1)
            m_ref[qi] = jnp.broadcast_to(top, m_ref.shape[1:])
            acc_ref[qi] = add
        longest = jnp.maximum(counts[0], counts[1])

        def body(g, carry):
            for b in (0, 1):
                qi = 2 * d + b
                fs, pads = slots_of(list_ref, qi, 2 + 4 * g, counts[b], 4)
                top, add = fwd_group(kv, vt, q2[b], fs, pads)
                merge(m_ref, acc_ref, qi, top, add)
            return carry

        lax.fori_loop(0, (longest + 1) // 4, body, 0)


def near(chunk, lists, counts, own0, rest0, own1, rest1, seconds):
    return pl.pallas_call(
        functools.partial(near_kernel, chunk),
        out_shape=(
            jax.ShapeDtypeStruct((8, 8, 256), F32),
            jax.ShapeDtypeStruct((8, 144, 256), F32),
        ),
        in_specs=[SMEM, SMEM] + [ANY] * 8,
        out_specs=[VMEM, VMEM],
        scratch_shapes=[
            pltpu.VMEM((32, BLOCK, LANES), BF16),
            pltpu.VMEM((32, 144, LANES), BF16),
            pltpu.VMEM((8, LANES, BLOCK), BF16),
            pltpu.SemaphoreType.DMA((8,)),
        ],
        compiler_params=params(),
        cost_estimate=pl.CostEstimate(flops=8_000_000_000, bytes_accessed=4_000_000, transcendentals=0),
        name=f"near{chunk}",
    )(lists, counts, own0, rest0, own1, rest1, *seconds)


def far_kernel(
    chunk, fast, me_ref, list_ref, count_ref, own2, rest2, s0, s1, s2, s3, go, m_in, acc_in, *refs
):
    if fast:
        attn_ref, lse_ref, w0, w1, w2, w3, m_ref, acc_ref, kv, vt, qt, go_v, wide, sem = refs
    else:
        attn_ref, lse_ref, w0, m_ref, acc_ref, kv, vt, qt, go_v, wide, sem = refs
    copies = row_copies(chunk, 256, 0, own2, rest2, kv, sem, 0)
    copies += query_copies(chunk, (s0, s1, s2, s3), qt, sem, 2)
    copies.append(pltpu.make_async_copy(m_in, m_ref, sem.at[6]))
    copies.append(pltpu.make_async_copy(acc_in, acc_ref, sem.at[7]))
    go_copy = pltpu.make_async_copy(go, go_v, sem.at[8])
    for copy in copies:
        copy.start()
    go_copy.start()
    for copy in copies:
        copy.wait()
    base = 8 * ROW
    turn_values(kv, vt, [base + 4 * i + b for i in range(ROW) for b in (0, 1)], base)
    for d in range(ROW):
        q2 = [block_diag(qt[2 * d + b]) for b in (0, 1)]
        starts = [count_ref[2 * d + b, 0] for b in (0, 1)]
        counts = [count_ref[2 * d + b, 1] for b in (0, 1)]
        longest = jnp.maximum(counts[0] - starts[0], counts[1] - starts[1])

        def body(g, carry):
            for b in (0, 1):
                qi = 2 * d + b
                fs, pads = slots_of(list_ref, qi, starts[b] + 4 * g, counts[b], 4, base)
                top, add = fwd_group(kv, vt, q2[b], fs, pads)
                merge(m_ref, acc_ref, qi, top, add)
            return carry

        lax.fori_loop(0, (longest + 3) // 4, body, 0)
    for qi in range(2 * ROW):
        total = acc_ref[qi, LANES : LANES + 1, :]
        lse_ref[qi] = m_ref[qi] + jnp.log(jnp.broadcast_to(total, m_ref.shape[1:]))
        out = pick_heads(acc_ref[qi, 0:LANES, :] / total)
        attn_ref[:, qi * BLOCK : (qi + 1) * BLOCK] = out.astype(BF16)
    go_copy.wait()
    wide[...] = nn(attn_ref[...], go_v[...])
    if fast:
        z = me_ref[1]
        half = LANES // 2
        for delta, w in enumerate((w0, w1, w2, w3)):
            target = (z + delta) % 4 - 2 * chunk
            inside = jnp.logical_and(target >= 0, target < 2)
            at = pl.multiple_of(jnp.where(inside, target, 0) * half, half)
            piece = wide[pl.ds(at, half), :]
            w[...] = jnp.where(inside, piece, 0.0).astype(BF16)
    else:
        w0[...] = wide[...].astype(BF16)


def far(chunk, fast, me, lists, counts, own2, rest2, seconds, go, m, acc):
    width = go.shape[1]
    weights = (
        (jax.ShapeDtypeStruct((LANES // 2, width), BF16),) * 4
        if fast
        else (jax.ShapeDtypeStruct((LANES, width), BF16),)
    )
    return pl.pallas_call(
        functools.partial(far_kernel, chunk, fast),
        out_shape=(
            jax.ShapeDtypeStruct((LANES, 8 * BLOCK), BF16),
            jax.ShapeDtypeStruct((8, 8, 256), F32),
        )
        + weights,
        in_specs=[SMEM, SMEM, SMEM] + [ANY] * 9,
        out_specs=[VMEM] * (2 + len(weights)),
        scratch_shapes=[
            pltpu.VMEM((8, 8, 256), F32),
            pltpu.VMEM((8, 144, 256), F32),
            pltpu.VMEM((16, BLOCK, LANES), BF16),
            pltpu.VMEM((16, 144, LANES), BF16),
            pltpu.VMEM((8, LANES, BLOCK), BF16),
            pltpu.VMEM(go.shape, BF16),
            pltpu.VMEM((LANES, width), F32),
            pltpu.SemaphoreType.DMA((9,)),
        ],
        compiler_params=params(),
        cost_estimate=pl.CostEstimate(flops=5_000_000_000, bytes_accessed=6_000_000, transcendentals=0),
        name=f"far{chunk}",
    )(me, lists, counts, own2, rest2, *seconds, go, m, acc)


def bwd_group(kv, kt, q2, g2, lse, delta, fs, pads, diag=None):
    keys = jnp.concatenate([kv[f] for f in fs], axis=0)
    values = jnp.concatenate([kv[f + 2] for f in fs], axis=0)
    scores = nn(keys, q2)
    dprob = nn(values, g2)
    probs, dscores = [], []
    for i, pad in enumerate(pads):
        part = scores[i * BLOCK : (i + 1) * BLOCK]
        if diag == i:
            part = jnp.where(causal(part.shape), part, NEG)
        prob = jnp.exp(part - (lse + pad))
        dscore = prob * (dprob[i * BLOCK : (i + 1) * BLOCK] - delta)
        probs.append(prob)
        dscores.append(dscore.astype(BF16))
    turned = jnp.concatenate([kt[f] for f in fs], axis=1)
    return probs, dscores, nn(turned, jnp.concatenate(dscores, axis=0))


def back_kernel(
    chunk, list_ref, count_ref, own0, rest0, own1, rest1, own2, rest2, s0, s1, s2, s3,
    gt_ref, attn_ref, lse_ref, o0, o1, o2, o3, kv, kt, qt, dq, sem,
):
    copies = row_copies(chunk, 256, 0, own0, rest0, kv, sem, 0)
    copies += row_copies(chunk, 256, 1, own1, rest1, kv, sem, 2)
    copies += row_copies(chunk, 256, 2, own2, rest2, kv, sem, 4)
    copies += query_copies(chunk, (s0, s1, s2, s3), qt, sem, 6)
    for copy in copies:
        copy.start()
    for copy in copies:
        copy.wait()
    for f in [4 * i + b for i in range(3 * ROW) for b in (0, 1)]:
        kt[f] = kv[f].astype(F32).T.astype(BF16)
    outs = (o0, o1, o2, o3)
    half = LANES // 2
    for d in range(ROW):
        q2, g2, lse, delta, counts = [], [], [], [], []
        for b in (0, 1):
            qi = 2 * d + b
            gt = gt_ref[:, qi * BLOCK : (qi + 1) * BLOCK]
            product = gt.astype(F32) * attn_ref[:, qi * BLOCK : (qi + 1) * BLOCK].astype(F32)
            delta.append(
                jnp.concatenate(
                    [
                        jnp.sum(product[:half], axis=0, keepdims=True),
                        jnp.sum(product[half:], axis=0, keepdims=True),
                    ],
                    axis=1,
                )
            )
            q2.append(block_diag(qt[qi]))
            g2.append(block_diag(gt))
            lse.append(lse_ref[qi, 0:1, :])
            counts.append(count_ref[qi, 1])
        local = []
        for b in (0, 1):
            qi = 2 * d + b
            fs, pads = slots_of(list_ref, qi, 0, counts[b], 2)
            fs = [4 * d, 4 * d + b] + fs
            pads = [jnp.float32(0.0 if b else PAD), jnp.float32(0.0)] + pads
            probs, dscores, add = bwd_group(
                kv, kt, q2[b], g2[b], lse[b], delta[b], fs, pads, diag=1
            )
            dq[b] = add
            local.append(([p.astype(BF16) for p in probs[:2]], dscores[:2]))
        q_both = jnp.concatenate(q2, axis=1)
        g_both = jnp.concatenate(g2, axis=1)
        out = outs[d]
        out[256:384, :] = nt(
            jnp.concatenate([local[0][1][1], local[1][1][0]], axis=1), q_both
        ).astype(BF16)
        out[384:512, :] = nt(local[1][1][1], q2[1]).astype(BF16)
        out[512:640, :] = nt(
            jnp.concatenate([local[0][0][1], local[1][0][0]], axis=1), g_both
        ).astype(BF16)
        out[640:768, :] = nt(local[1][0][1], g2[1]).astype(BF16)
        longest = jnp.maximum(counts[0], counts[1])

        def body(g, carry):
            for b in (0, 1):
                qi = 2 * d + b
                fs, pads = slots_of(list_ref, qi, 2 + 4 * g, counts[b], 4)
                _, _, add = bwd_group(kv, kt, q2[b], g2[b], lse[b], delta[b], fs, pads)
                dq[b] += add
            return carry

        lax.fori_loop(0, (longest + 1) // 4, body, 0)
        for b in (0, 1):
            grad = pick_heads(dq[b]) * 0.125
            out[b * BLOCK : (b + 1) * BLOCK, :] = grad.T.astype(BF16)


def back(chunk, lists, counts, row0, row1, row2, seconds, gt, attn, lse):
    return pl.pallas_call(
        functools.partial(back_kernel, chunk),
        out_shape=(jax.ShapeDtypeStruct((768, LANES), BF16),) * 4,
        in_specs=[SMEM, SMEM] + [ANY] * 10 + [VMEM] * 3,
        out_specs=[VMEM] * 4,
        scratch_shapes=[
            pltpu.VMEM((48, BLOCK, LANES), BF16),
            pltpu.VMEM((48, LANES, BLOCK), BF16),
            pltpu.VMEM((8, LANES, BLOCK), BF16),
            pltpu.VMEM((2, LANES, 256), F32),
            pltpu.SemaphoreType.DMA((10,)),
        ],
        compiler_params=params(),
        cost_estimate=pl.CostEstimate(flops=10_000_000_000, bytes_accessed=8_000_000, transcendentals=0),
        name=f"back{chunk}",
    )(lists, counts, *row0, *row1, *row2, *seconds, gt, attn, lse)


def unpack_kernel(me_ref, *refs):
    ins, outs = refs[:8], refs[8:]
    r = me_ref[0]
    odd_me = (r % 2) == 1
    rows = outs[0].shape[0]
    for chunk in (0, 1):
        for pair in (0, 1):
            tile = 4 * chunk + (r // 2 + pair) % 2
            first, second = ins[4 * chunk + 2 * pair], ins[4 * chunk + 2 * pair + 1]
            for which, out in enumerate(outs):
                a = first[which * rows : (which + 1) * rows, :].astype(F32)
                b = second[which * rows : (which + 1) * rows, :].astype(F32)
                low, high = jnp.where(odd_me, b, a), jnp.where(odd_me, a, b)
                one, two = split_pair(low, high)
                at = pl.multiple_of(tile * LANES, LANES)
                out[:, pl.ds(at, LANES)] = one.astype(BF16)
                at = pl.multiple_of((tile + 2) * LANES, LANES)
                out[:, pl.ds(at, LANES)] = two.astype(BF16)


def unpack(me, pieces, rows, width):
    return pl.pallas_call(
        unpack_kernel,
        out_shape=(jax.ShapeDtypeStruct((rows, width), BF16),) * 3,
        in_specs=[SMEM] + [VMEM] * 8,
        out_specs=[VMEM] * 3,
        compiler_params=params(),
        name="unpack",
    )(me, *pieces)


def swap(value, axis, bit):
    count = lax.axis_size(axis)
    return lax.ppermute(value, axis, [(s, s ^ bit) for s in range(count)])


def later(value, axis):
    count = lax.axis_size(axis)
    return lax.ppermute(value, axis, [(s, s + ROW) for s in range(count - ROW)])


def shards(queries, keys, values, track, out_weight, grad_out):
    rows, width = queries.shape
    count = lax.axis_size("span")
    index = lax.axis_index("span").astype(jnp.int32)
    r, z = index % ROW, index // ROW
    me = jnp.stack([r, z])
    fast = count == HEADS
    track_block = jnp.pad(track.astype(BF16), ((0, 14), (0, LANES - track.shape[1])))
    own0, firsts, seconds = pack(me, queries, keys, values, track_block)

    own1 = later(own0, "span")
    got_first = [swap(firsts[d], "span", d) for d in (1, 2, 3)]
    got_second = [swap(seconds[d], "span", d) for d in (1, 2, 3)]
    own2 = later(own1, "span")
    seconds = [seconds[0]] + got_second
    rest0 = [
        jnp.concatenate(got_first, axis=0),
        jnp.concatenate([x[: 2 * rows] for x in got_second], axis=0),
    ]
    rest1 = [later(x, "span") for x in rest0]
    rest2 = [later(x, "span") for x in rest1]

    go2 = swap(grad_out, "span", 2)
    go1 = swap(grad_out, "span", 1)
    go3 = swap(go2, "span", 1)
    go = jnp.concatenate([grad_out, go1, go2, go3], axis=0)

    track_row = jnp.concatenate([x[4 * rows : 4 * rows + 2, : 2 * WINDOW] for x in seconds], axis=0)
    lists, counts = plan(me, track_row.astype(jnp.int32))

    head_dim = width // HEADS
    weight_rows = lax.dynamic_index_in_dim(
        out_weight.reshape(ROW, ROW, head_dim, width), r, 1, keepdims=False
    ).reshape(ROW * head_dim, width)
    grad_turned = lax.dot_general(
        weight_rows, go, (((1,), (1,)), ((), ())), preferred_element_type=F32
    ).astype(BF16)

    states, pieces, weights = [], [], []
    for chunk in (0, 1):
        states.append(near(chunk, lists, counts, own0, rest0[chunk], own1, rest1[chunk], seconds))
    for chunk in (0, 1):
        attn, lse, *terms = far(
            chunk, fast, me, lists, counts, own2, rest2[chunk], seconds, go, *states[chunk]
        )
        if fast:
            received = [terms[0].astype(F32)]
            for delta in (1, 2, 3):
                pairs = [
                    (ROW * s + q, ROW * ((s + delta) % ROW) + q)
                    for s in range(ROW)
                    for q in range(ROW)
                    if (s + delta) % ROW // 2 == chunk
                ]
                received.append(lax.ppermute(terms[delta], "span", pairs).astype(F32))
            weights += received
        else:
            weights.append(terms[0])
        out = back(
            chunk,
            lists,
            counts,
            (own0, rest0[chunk]),
            (own1, rest1[chunk]),
            (own2, rest2[chunk]),
            seconds,
            grad_turned[chunk * LANES : (chunk + 1) * LANES],
            attn,
            lse,
        )
        pieces.append(out[0])
        pieces += [swap(out[d], "span", d) for d in (1, 2, 3)]
    query_grad, key_grad, value_grad = unpack(me, pieces, rows, width)
    if fast:
        weight_grad = functools.reduce(lambda a, b: a + b, weights)
    else:
        mine = jnp.concatenate(weights, axis=0).reshape(ROW, 1, head_dim, width)
        full = jnp.zeros((ROW, ROW, head_dim, width), BF16)
        full = lax.dynamic_update_slice(full, mine, (0, r, 0, 0)).reshape(width, width)
        weight_grad = lax.psum_scatter(full.astype(F32), "span", scatter_dimension=0, tiled=True)
    return (query_grad, key_grad, value_grad, weight_grad)


def solution(mesh):
    spec = P(("groups", "span"), None)
    return jax.shard_map(
        shards,
        mesh=mesh,
        in_specs=(spec, spec, spec, spec, P(), spec),
        out_specs=(spec, spec, spec, spec),
        check_vma=False,
    )
```

time: 521 us -> 156 us (0.30)
  waiting for transfers between devices: 280 us -> 31 us
  matrix products: 85 us -> 0.75 us
  local copies, waits for them, and re-layouts: 75.6 us -> 14.4 us
  Pallas kernels: 0 us -> 58.4 us
  other arithmetic: 30.6 us -> 2.4 us
  starting transfers between devices: 27.9 us -> 45.8 us
  between operations: 14.2 us -> 1.13 us
    reduce_scatter x1 -> x0, waiting for transfers between devices: 156 us -> none  [shards(): lax.psum_scatter(lax.dot_general(attn_out, grad_out, (((0,), (0,)), ((),...]
    ppermute x8 -> x27, waiting for transfers between devices: 124 us -> 31 us  [the longest x15 23.3 us: swap(): return lax.ppermute(value, axis, [(s, s ^ bit) for s in range(count)])]
    pallas_call x0 -> x9, Pallas kernels: none -> 58.4 us  [the longest x2 22.5 us: near(): pl.pallas_call(functools.partial(near_kernel, chunk), out_shape=(jax.Shap...]
    dot_general x42 -> x1, matrix products: 45.1 us -> 0.75 us  [shards(): lax.dot_general(weight_rows, go, (((1,), (1,)), ((), ())), preferred_elem...]
    sub x8 -> x0, matrix products: 39.9 us -> none  [pair_grads(): expo = jnp.exp(scores - top)]
    dynamic_slice x48 -> x1, local copies, waits for them, and re-layouts: 33 us -> 0.84 us  [shards(): lax.dynamic_index_in_dim(out_weight.reshape(ROW, ROW, head_dim, width), r...]
    convert_element_type x8 -> x2, other arithmetic: 24 us -> 1.43 us  [the longest x1 0.83 us: shards(): track.astype(BF16)]
    dynamic_update_slice x48 -> x0, local copies, waits for them, and re-layouts: 18.3 us -> none  [the longest x16 6.28 us: head_pair(): lax.dynamic_update_slice_in_dim(value_buf, value_g.reshape(rows, pair_wid...]
  transfers between devices with their start and end apart: 9 -> 27, of which waited for: 8 -> 6; matrix products, arithmetic and copies ran while one was open for 3% -> 6% of each run, Pallas kernels for 0% -> 35%
where the time goes in v1:
time: 156 us; the launch traced here: 154 us
  Pallas kernels  58.4 us (37%)
  starting transfers between devices  45.8 us (29%)
  waiting for transfers between devices  31 us (20%)
  local copies, waits for them, and re-layouts  14.4 us (9%)
  other arithmetic  2.4 us (2%)
    ppermute x15, waiting for transfers between devices, swap(): return lax.ppermute(value, axis, [(s, s ^ bit) for s in range(count)])  23.3 us
    pallas_call x2, Pallas kernels, near(): pl.pallas_call(functools.partial(near_kernel, chunk), out_shape=(jax.Shap...  22.5 us
    pallas_call x2, Pallas kernels, back(): pl.pallas_call(functools.partial(back_kernel, chunk), out_shape=(jax.Shap...  20.6 us
    ppermute x6, starting transfers between devices, later(): return lax.ppermute(value, axis, [(s, s + ROW) for s in range(count - ROW)])  16.6 us
    ppermute x15, starting transfers between devices, swap(): return lax.ppermute(value, axis, [(s, s ^ bit) for s in range(count)])  14.7 us
    ppermute x6, starting transfers between devices, shards(): received.append(lax.ppermute(terms[delta], 'span', pairs).astype(F32))  14.5 us
    unnamed x37, local copies, waits for them, and re-layouts  12.7 us
    ppermute x6, waiting for transfers between devices, shards(): received.append(lax.ppermute(terms[delta], 'span', pairs).astype(F32))  7.74 us
  transfers between devices with their start and end apart: 27, of which 6 were waited for; matrix products, arithmetic and copies ran while one was open for 6% of the time, Pallas kernels for 35%

profile of v1, /device:TPU:11, one launch (start us, length us, event | category | flops | bytes accessed | tf_op | source)
XLA Modules:
  0.0 153.9 jit_solution(883501602065497049)
XLA Ops:
  0.6 0.0 copy-start
  0.7 0.8 convert_element_type.35
  1.5 0.1 pad_add_fusion.me_ref
  1.6 1.0 copy-done.1
  2.6 1.0 copy-done.2
  3.7 1.0 copy-done.3
  4.7 2.3 %pack.1 = (bf16[1024,128]{1,0:T(8,128)(2,1)S(1)}, bf16[512,128]{1,0:T(8,128)(2,1)}, bf16[512,128]{1,0:T(8,128)(2,1)S(1)}, bf16[512,128]{1,0:T(8,128)(2,1)}, bf16...) custom-call(s32[2]{0:T(128)S(1)} %pad_add_fusion.me_ref, ...), custom_call_target="tpu_custom_call" | custom-call | tf_op jit(solution)/shard_map/pack/pallas_call | solution.py:88
  7.0 0.7 copy-done.7
  7.7 0.7 collective-permute-start.3
  8.4 1.1 collective-permute-start.2
  9.5 0.2 collective-permute-start.1
  9.8 0.8 collective-permute-start
  10.6 1.2 collective-permute-start.4
  11.8 1.9 %constant_dynamic-update-slice_fusion.6 = bf16[1024,1024]{1,0:T(8,128)(2,1)} fusion(bf16[256,1024]{1,0:T(8,128)(2,1)} %param.11), kind=kLoop, calls=%fused_computation.9 | loop fusion | bytes 1048576
  13.7 0.7 copy-done.15
  14.3 0.4 collective-permute-start.5
  14.7 0.9 constant_dynamic-update-slice_fusion.2
  15.6 9.3 %collective-permute-done.4 = bf16[512,128]{1,0:T(8,128)(2,1)} collective-permute-done((bf16[512,128]{1,0:T(8,128)(2,1)}, bf16[512,128]{1,0:T(8,128)(2,1)}, u32[]{:S(2)}, u32[]{:S(2)}) %collective-permute-start.4) | collective-permute-done | bytes 131104 | tf_op jit(solution)/shard_map/ppermute | solution.py:514
  24.9 3.2 %collective-permute-start.6 = (bf16[1024,128]{1,0:T(8,128)(2,1)S(1)}, bf16[1024,128]{1,0:T(8,128)(2,1)}, u32[]{:S(2)}, u32[]{:S(2)}) collective-permute-start(bf16[1024,128]{1,0:T(8,128)(2,1)S(1)} %get-tuple-element.47.own0), channel_id=1, source_target_pairs={{0,4},{1,5},{2,6},{3,7},{4,8},{5,9},{6,10},{7,11},{8,12},{9,13},{1... | collective-permute-start | bytes 786440 | tf_op jit(solution)/shard_map/ppermute | solution.py:519
  28.1 0.9 constant_dynamic-update-slice_fusion.1
  29.0 1.3 collective-permute-start.11
  30.4 3.2 %collective-permute-start.7 = (bf16[1536,128]{1,0:T(8,128)(2,1)S(1)}, bf16[1536,128]{1,0:T(8,128)(2,1)}, u32[]{:S(2)}, u32[]{:S(2)}) collective-permute-start(bf16[1536,128]{1,0:T(8,128)(2,1)S(1)} %constant_dynamic-update-slice_fusion.rest0), channel_id=1, source_target_pairs={{0,4},{1,5},{2,6},{3,7},{4,8},{5,9},{6,10},{7,11},{8,12},{9,13},{1... | collective-permute-start | bytes 1179656 | tf_op jit(solution)/shard_map/ppermute | solution.py:519
  33.6 0.8 constant_dynamic-slice_fusion
  34.4 0.7 slice.27
  35.1 2.5 %collective-permute-start.10 = (bf16[256,1024]{1,0:T(8,128)(2,1)}, bf16[256,1024]{1,0:T(8,128)(2,1)}, u32[]{:S(2)}, u32[]{:S(2)}) collective-permute-start(bf16[256,1024]{1,0:T(8,128)(2,1)} %param.11), channel_id=1, source_target_pairs={{0,1},{1,0},{2,3},{3,2},{4,5},{5,4},{6,7},{7,6},{8,9},{9,8},{10,11... | collective-permute-start | bytes 1572872 | tf_op jit(solution)/shard_map/ppermute | solution.py:514
  37.6 1.9 %collective-permute-start.8 = (bf16[1024,128]{1,0:T(8,128)(2,1)}, bf16[1024,128]{1,0:T(8,128)(2,1)}, u32[]{:S(2)}, u32[]{:S(2)}) collective-permute-start(bf16[1024,128]{1,0:T(8,128)(2,1)} %collective-permute-done.6.own1), channel_id=1, source_target_pairs={{0,4},{1,5},{2,6},{3,7},{4,8},{5,9},{6,10},{7,11},{8,12},{9,13},{1... | collective-permute-start | bytes 786440 | tf_op jit(solution)/shard_map/ppermute | solution.py:519
  39.6 0.6 maximum_convert_fusion.track_ref
  40.2 5.1 %plan.1 = (s32[8,24]{1,0:T(8,128)}, s32[8,2]{1,0:T(8,128)}) custom-call(s32[2]{0:T(128)} %copy-done.5, s32[8,16]{1,0:T(8,128)} %maximum_convert_fusion.track_ref), custom_call_target="tpu_custom_call" | custom-call | tf_op jit(solution)/shard_map/plan/pallas_call | solution.py:139
  45.4 3.7 %collective-permute-start.16 = (bf16[1536,128]{1,0:T(8,128)(2,1)S(1)}, bf16[1536,128]{1,0:T(8,128)(2,1)S(1)}, u32[]{:S(2)}, u32[]{:S(2)}) collective-permute-start(bf16[1536,128]{1,0:T(8,128)(2,1)S(1)} %pad_maximum_fusion.rest0), channel_id=1, source_target_pairs={{0,4},{1,5},{2,6},{3,7},{4,8},{5,9},{6,10},{7,11},{8,12},{9,13},{1... | collective-permute-start | bytes 1179656 | tf_op jit(solution)/shard_map/ppermute | solution.py:519
  49.1 1.9 %collective-permute-start.9 = (bf16[1536,128]{1,0:T(8,128)(2,1)}, bf16[1536,128]{1,0:T(8,128)(2,1)S(1)}, u32[]{:S(2)}, u32[]{:S(2)}) collective-permute-start(bf16[1536,128]{1,0:T(8,128)(2,1)} %collective-permute-done.7.rest1), channel_id=1, source_target_pairs={{0,4},{1,5},{2,6},{3,7},{4,8},{5,9},{6,10},{7,11},{8,12},{9,13},{1... | collective-permute-start | bytes 1179656 | tf_op jit(solution)/shard_map/ppermute | solution.py:519
  51.0 0.6 collective-permute-start.12
  51.6 0.9 copy-done.8
  52.6 0.7 copy-done.10
  53.3 0.7 copy-done.12
  54.0 11.2 %near0.1 = (f32[8,8,256]{2,1,0:T(8,128)S(1)}, f32[8,144,256]{2,1,0:T(8,128)S(1)}) custom-call(s32[8,24]{1,0:T(8,128)S(1)} %copy-done.10, s32[8,2]{1,0:T(8,128)S(1)} %copy-done.12, bf16[1024,128]{1,0:T(8,128)(2,1)S(1)} %get-tuple-element.47.own0, bf16[1536,128]{1,0:T(8,128)(2,1)S(1)} %constant_dynamic-update-slice_fusion.rest0, ...), custom_call_target="tpu_custom_call" | custom-call | flops 8000000000 | bytes 4000000 | tf_op jit(solution)/shard_map/near0/pallas_call | solution.py:265
  65.2 1.1 constant_dynamic-update-slice_fusion.5
  66.4 1.1 constant_dynamic-update-slice_fusion.4
  67.5 2.7 %collective-permute-start.17 = (bf16[1536,128]{1,0:T(8,128)(2,1)S(1)}, bf16[1536,128]{1,0:T(8,128)(2,1)S(1)}, u32[]{:S(2)}, u32[]{:S(2)}) collective-permute-start(bf16[1536,128]{1,0:T(8,128)(2,1)S(1)} %collective-permute-done.16.rest1), channel_id=1, source_target_pairs={{0,4},{1,5},{2,6},{3,7},{4,8},{5,9},{6,10},{7,11},{8,12},{9,13},{1... | collective-permute-start | bytes 1179656 | tf_op jit(solution)/shard_map/ppermute | solution.py:519
  70.2 11.3 %near1.1 = (f32[8,8,256]{2,1,0:T(8,128)S(1)}, f32[8,144,256]{2,1,0:T(8,128)S(1)}) custom-call(s32[8,24]{1,0:T(8,128)S(1)} %copy-done.10, s32[8,2]{1,0:T(8,128)S(1)} %copy-done.12, bf16[1024,128]{1,0:T(8,128)(2,1)S(1)} %get-tuple-element.47.own0, bf16[1536,128]{1,0:T(8,128)(2,1)S(1)} %pad_maximum_fusion.rest0, bf16[1024,128]{1,0:T(8,128)(2,1)} %collective-permute-done.6.own1, ...), custom_call_target="tpu_custom_call" | custom-call | flops 8000000000 | bytes 4000000 | tf_op jit(solution)/shard_map/near1/pallas_call | solution.py:265
  81.5 0.0 copy-start.11
  81.5 0.7 convolution_convert_fusion
  82.4 2.6 %far0.1 = (bf16[128,1024]{1,0:T(8,128)(2,1)S(1)}, f32[8,8,256]{2,1,0:T(8,128)S(1)}, bf16[64,1024]{1,0:T(8,128)(2,1)S(1)}, bf16[64,1024]{1,0:T(8,128)(2,1)S(1)}, ...) custom-call(s32[2]{0:T(128)S(1)} %copy-done.6, s32[8,24]{1,0:T(8,128)S(1)} %copy-done.11, ...), custom_call_target="tpu_custom_call" | custom-call | flops 5000000000 | bytes 6000000 | tf_op jit(solution)/shard_map/far0/pallas_call | solution.py:346
  85.0 10.3 %back0.1 = (bf16[768,128]{1,0:T(8,128)(2,1)S(1)}, bf16[768,128]{1,0:T(8,128)(2,1)S(1)}, bf16[768,128]{1,0:T(8,128)(2,1)S(1)}, bf16[768,128]{1,0:T(8,128)(2,1)S(1)}) custom-call(s32[8,24]{1,0:T(8,128)S(1)} %copy-done.11, s32[8,2]{1,0:T(8,128)S(1)} %copy-done.13, bf16[1024,128]{1,0:T(8,128)(2,1)S(1)} %get-tuple-element.47.own0, ...), custom_call_target="tpu_custom_call" | custom-call | flops 10000000000 | bytes 8000000 | tf_op jit(solution)/shard_map/back0/pallas_call | solution.py:463
  95.3 0.5 collective-permute-start.13
  95.9 1.9 %collective-permute-start.23 = (bf16[64,1024]{1,0:T(8,128)(2,1)S(1)}, bf16[64,1024]{1,0:T(8,128)(2,1)S(1)}, u32[]{:S(2)}, u32[]{:S(2)}) collective-permute-start(bf16[64,1024]{1,0:T(8,128)(2,1)S(1)} %get-tuple-element.73), channel_id=1, source_target_pairs={{4,0},{5,1},{6,2},{7,3},{8,4},{9,5},{10,6},{11,7},{20,16},{21,17},... | collective-permute-start | bytes 393224 | tf_op jit(solution)/shard_map/ppermute | solution.py:576
  97.8 1.3 collective-permute-start.22
  99.1 1.3 collective-permute-start.21
  100.4 2.9 %far1.1 = (bf16[128,1024]{1,0:T(8,128)(2,1)S(1)}, f32[8,8,256]{2,1,0:T(8,128)S(1)}, bf16[64,1024]{1,0:T(8,128)(2,1)S(1)}, bf16[64,1024]{1,0:T(8,128)(2,1)S(1)}, ...) custom-call(s32[2]{0:T(128)S(1)} %copy-done.6, s32[8,24]{1,0:T(8,128)S(1)} %copy-done.11, ...), custom_call_target="tpu_custom_call" | custom-call | flops 5000000000 | bytes 6000000 | tf_op jit(solution)/shard_map/far1/pallas_call | solution.py:346
  103.3 0.7 collective-permute-start.26
  104.0 7.7 %collective-permute-done.23 = bf16[64,1024]{1,0:T(8,128)(2,1)S(1)} collective-permute-done((bf16[64,1024]{1,0:T(8,128)(2,1)S(1)}, bf16[64,1024]{1,0:T(8,128)(2,1)S(1)}, u32[]{:S(2)}, u32[]{:S(2)}) %collective-permute-start.23) | collective-permute-done | bytes 131104 | tf_op jit(solution)/shard_map/ppermute | solution.py:576
  111.7 8.0 %collective-permute-start.25 = (bf16[64,1024]{1,0:T(8,128)(2,1)S(1)}, bf16[64,1024]{1,0:T(8,128)(2,1)S(1)}, u32[]{:S(2)}, u32[]{:S(2)}) collective-permute-start(bf16[64,1024]{1,0:T(8,128)(2,1)S(1)} %get-tuple-element.76), channel_id=1, source_target_pairs={{0,8},{1,9},{2,10},{3,11},{4,12},{5,13},{6,14},{7,15},{16,24},{17,... | collective-permute-start | bytes 393224 | tf_op jit(solution)/shard_map/ppermute | solution.py:576
  119.7 1.3 collective-permute-start.24
  121.1 10.3 %back1.1 = (bf16[768,128]{1,0:T(8,128)(2,1)S(1)}, bf16[768,128]{1,0:T(8,128)(2,1)S(1)}, bf16[768,128]{1,0:T(8,128)(2,1)S(1)}, bf16[768,128]{1,0:T(8,128)(2,1)S(1)}) custom-call(s32[8,24]{1,0:T(8,128)S(1)} %copy-done.11, s32[8,2]{1,0:T(8,128)S(1)} %copy-done.13, bf16[1024,128]{1,0:T(8,128)(2,1)S(1)} %get-tuple-element.47.own0, ...), custom_call_target="tpu_custom_call" | custom-call | flops 10000000000 | bytes 8000000 | tf_op jit(solution)/shard_map/back1/pallas_call | solution.py:463
  131.4 2.3 %collective-permute-start.14 = (bf16[768,128]{1,0:T(8,128)(2,1)S(1)}, bf16[768,128]{1,0:T(8,128)(2,1)S(1)}, u32[]{:S(2)}, u32[]{:S(2)}) collective-permute-start(bf16[768,128]{1,0:T(8,128)(2,1)S(1)} %get-tuple-element.57), channel_id=1, source_target_pairs={{0,2},{1,3},{2,0},{3,1},{4,6},{5,7},{6,4},{7,5},{8,10},{9,11},{10,... | collective-permute-start | bytes 589832 | tf_op jit(solution)/shard_map/ppermute | solution.py:514
  133.7 0.8 collective-permute-start.15
  134.5 0.4 collective-permute-start.18
  134.9 1.4 collective-permute-start.19
  136.2 0.4 collective-permute-start.20
  136.6 0.9 convert_add_fusion
  137.5 0.6 collective-permute-done.14.refs_2_
  138.1 5.9 %collective-permute-done.15.refs_3_ = bf16[768,128]{1,0:T(8,128)(2,1)S(1)} collective-permute-done((bf16[768,128]{1,0:T(8,128)(2,1)S(1)}, bf16[768,128]{1,0:T(8,128)(2,1)S(1)}, u32[]{:S(2)}, u32[]{:S(2)}) %collective-permute-start.15) | collective-permute-done | bytes 196640 | tf_op jit(solution)/shard_map/ppermute | solution.py:514
  144.1 2.5 %collective-permute-done.19.refs_6_ = bf16[768,128]{1,0:T(8,128)(2,1)S(1)} collective-permute-done((bf16[768,128]{1,0:T(8,128)(2,1)S(1)}, bf16[768,128]{1,0:T(8,128)(2,1)S(1)}, u32[]{:S(2)}, u32[]{:S(2)}) %collective-permute-start.19) | collective-permute-done | bytes 196640 | tf_op jit(solution)/shard_map/ppermute | solution.py:514
  146.6 4.9 %collective-permute-done.20.refs_7_ = bf16[768,128]{1,0:T(8,128)(2,1)S(1)} collective-permute-done((bf16[768,128]{1,0:T(8,128)(2,1)S(1)}, bf16[768,128]{1,0:T(8,128)(2,1)S(1)}, u32[]{:S(2)}, u32[]{:S(2)}) %collective-permute-start.20) | collective-permute-done | bytes 196640 | tf_op jit(solution)/shard_map/ppermute | solution.py:514
  151.5 2.4 %unpack.1 = (bf16[256,1024]{1,0:T(8,128)(2,1)}, bf16[256,1024]{1,0:T(8,128)(2,1)}, bf16[256,1024]{1,0:T(8,128)(2,1)}) custom-call(s32[2]{0:T(128)S(1)} %copy-done.6, bf16[768,128]{1,0:T(8,128)(2,1)S(1)} %get-tuple-element.55.refs_0_, bf16[768,128]{1,0:T(8,128)(2,1)S(1)} %collective-permute-done.13.refs_1_, ...), custom_call_target="tpu_custom_call" | custom-call | tf_op jit(solution)/shard_map/unpack/pallas_call | solution.py:502
  (54 shorter events, 0.3 us)
Async XLA Ops:
  0.6 33.0 %copy-start = (bf16[1024,1024]{1,0:T(8,128)(2,1)S(1)}, bf16[1024,1024]{1,0:T(8,128)(2,1)}, u32[]{:S(2)}) copy-start(bf16[1024,1024]{1,0:T(8,128)(2,1)} %param.10) | copy-start | bytes 6291460
  1.6 32.9 %copy-start.5 = (s32[2]{0:T(128)}, s32[2]{0:T(128)S(1)}, u32[]{:S(2)}) copy-start(s32[2]{0:T(128)S(1)} %pad_add_fusion.me_ref) | copy-start | bytes 28
  1.6 1.0 copy-start.1
  2.6 1.0 copy-start.2
  3.7 1.0 copy-start.3
  7.0 0.7 copy-start.7
  7.7 5.9 %collective-permute-start.3 = (bf16[512,128]{1,0:T(8,128)(2,1)S(1)}, bf16[512,128]{1,0:T(8,128)(2,1)S(1)}, u32[]{:S(2)}, u32[]{:S(2)}) collective-permute-start(bf16[512,128]{1,0:T(8,128)(2,1)S(1)} %get-tuple-element.48), channel_id=1, source_target_pairs={{0,1},{1,0},{2,3},{3,2},{4,5},{5,4},{6,7},{7,6},{8,9},{9,8},{10,11... | collective-permute-start | bytes 393224 | tf_op jit(solution)/shard_map/ppermute | solution.py:514
  8.4 22.0 %collective-permute-start.2 = (bf16[1040,128]{1,0:T(8,128)(2,1)}, bf16[1040,128]{1,0:T(8,128)(2,1)S(1)}, u32[]{:S(2)}, u32[]{:S(2)}) collective-permute-start(bf16[1040,128]{1,0:T(8,128)(2,1)} %get-tuple-element.44), channel_id=1, source_target_pairs={{0,3},{1,2},{2,1},{3,0},{4,7},{5,6},{6,5},{7,4},{8,11},{9,10},{10,... | collective-permute-start | bytes 798728 | tf_op jit(solution)/shard_map/ppermute | solution.py:514
  9.5 28.1 %collective-permute-start.1 = (bf16[1040,128]{1,0:T(8,128)(2,1)}, bf16[1040,128]{1,0:T(8,128)(2,1)S(1)}, u32[]{:S(2)}, u32[]{:S(2)}) collective-permute-start(bf16[1040,128]{1,0:T(8,128)(2,1)} %get-tuple-element.43), channel_id=1, source_target_pairs={{0,2},{1,3},{2,0},{3,1},{4,6},{5,7},{6,4},{7,5},{8,10},{9,11},{10,... | collective-permute-start | bytes 798728 | tf_op jit(solution)/shard_map/ppermute | solution.py:514
  9.8 29.8 %collective-permute-start = (bf16[1040,128]{1,0:T(8,128)(2,1)}, bf16[1040,128]{1,0:T(8,128)(2,1)S(1)}, u32[]{:S(2)}, u32[]{:S(2)}) collective-permute-start(bf16[1040,128]{1,0:T(8,128)(2,1)} %get-tuple-element.42), channel_id=1, source_target_pairs={{0,1},{1,0},{2,3},{3,2},{4,5},{5,4},{6,7},{7,6},{8,9},{9,8},{10,11... | collective-permute-start | bytes 798728 | tf_op jit(solution)/shard_map/ppermute | solution.py:514
  10.6 14.3 %collective-permute-start.4 = (bf16[512,128]{1,0:T(8,128)(2,1)}, bf16[512,128]{1,0:T(8,128)(2,1)}, u32[]{:S(2)}, u32[]{:S(2)}) collective-permute-start(bf16[512,128]{1,0:T(8,128)(2,1)} %get-tuple-element.49), channel_id=1, source_target_pairs={{0,2},{1,3},{2,0},{3,1},{4,6},{5,7},{6,4},{7,5},{8,10},{9,11},{10,... | collective-permute-start | bytes 393224 | tf_op jit(solution)/shard_map/ppermute | solution.py:514
  13.7 0.7 copy-start.15
  14.3 14.7 %collective-permute-start.5 = (bf16[512,128]{1,0:T(8,128)(2,1)}, bf16[512,128]{1,0:T(8,128)(2,1)S(1)}, u32[]{:S(2)}, u32[]{:S(2)}) collective-permute-start(bf16[512,128]{1,0:T(8,128)(2,1)} %get-tuple-element.50), channel_id=1, source_target_pairs={{0,3},{1,2},{2,1},{3,0},{4,7},{5,6},{6,5},{7,4},{8,11},{9,10},{10,... | collective-permute-start | bytes 393224 | tf_op jit(solution)/shard_map/ppermute | solution.py:514
  24.9 10.2 %collective-permute-start.6 = (bf16[1024,128]{1,0:T(8,128)(2,1)S(1)}, bf16[1024,128]{1,0:T(8,128)(2,1)}, u32[]{:S(2)}, u32[]{:S(2)}) collective-permute-start(bf16[1024,128]{1,0:T(8,128)(2,1)S(1)} %get-tuple-element.47.own0), channel_id=1, source_target_pairs={{0,4},{1,5},{2,6},{3,7},{4,8},{5,9},{6,10},{7,11},{8,12},{9,13},{1... | collective-permute-start | bytes 786440 | tf_op jit(solution)/shard_map/ppermute | solution.py:519
  29.0 22.0 %collective-permute-start.11 = (bf16[256,1024]{1,0:T(8,128)(2,1)}, bf16[256,1024]{1,0:T(8,128)(2,1)}, u32[]{:S(2)}, u32[]{:S(2)}) collective-permute-start(bf16[256,1024]{1,0:T(8,128)(2,1)} %param.11), channel_id=1, source_target_pairs={{0,2},{1,3},{2,0},{3,1},{4,6},{5,7},{6,4},{7,5},{8,10},{9,11},{10,... | collective-permute-start | bytes 1572872 | tf_op jit(solution)/shard_map/ppermute | solution.py:514
  30.4 18.7 %collective-permute-start.7 = (bf16[1536,128]{1,0:T(8,128)(2,1)S(1)}, bf16[1536,128]{1,0:T(8,128)(2,1)}, u32[]{:S(2)}, u32[]{:S(2)}) collective-permute-start(bf16[1536,128]{1,0:T(8,128)(2,1)S(1)} %constant_dynamic-update-slice_fusion.rest0), channel_id=1, source_target_pairs={{0,4},{1,5},{2,6},{3,7},{4,8},{5,9},{6,10},{7,11},{8,12},{9,13},{1... | collective-permute-start | bytes 1179656 | tf_op jit(solution)/shard_map/ppermute | solution.py:519
  35.1 30.1 %collective-permute-start.10 = (bf16[256,1024]{1,0:T(8,128)(2,1)}, bf16[256,1024]{1,0:T(8,128)(2,1)}, u32[]{:S(2)}, u32[]{:S(2)}) collective-permute-start(bf16[256,1024]{1,0:T(8,128)(2,1)} %param.11), channel_id=1, source_target_pairs={{0,1},{1,0},{2,3},{3,2},{4,5},{5,4},{6,7},{7,6},{8,9},{9,8},{10,11... | collective-permute-start | bytes 1572872 | tf_op jit(solution)/shard_map/ppermute | solution.py:514
  37.6 44.7 %collective-permute-start.8 = (bf16[1024,128]{1,0:T(8,128)(2,1)}, bf16[1024,128]{1,0:T(8,128)(2,1)}, u32[]{:S(2)}, u32[]{:S(2)}) collective-permute-start(bf16[1024,128]{1,0:T(8,128)(2,1)} %collective-permute-done.6.own1), channel_id=1, source_target_pairs={{0,4},{1,5},{2,6},{3,7},{4,8},{5,9},{6,10},{7,11},{8,12},{9,13},{1... | collective-permute-start | bytes 786440 | tf_op jit(solution)/shard_map/ppermute | solution.py:519
  45.4 22.1 %collective-permute-start.16 = (bf16[1536,128]{1,0:T(8,128)(2,1)S(1)}, bf16[1536,128]{1,0:T(8,128)(2,1)S(1)}, u32[]{:S(2)}, u32[]{:S(2)}) collective-permute-start(bf16[1536,128]{1,0:T(8,128)(2,1)S(1)} %pad_maximum_fusion.rest0), channel_id=1, source_target_pairs={{0,4},{1,5},{2,6},{3,7},{4,8},{5,9},{6,10},{7,11},{8,12},{9,13},{1... | collective-permute-start | bytes 1179656 | tf_op jit(solution)/shard_map/ppermute | solution.py:519
  49.1 33.3 %collective-permute-start.9 = (bf16[1536,128]{1,0:T(8,128)(2,1)}, bf16[1536,128]{1,0:T(8,128)(2,1)S(1)}, u32[]{:S(2)}, u32[]{:S(2)}) collective-permute-start(bf16[1536,128]{1,0:T(8,128)(2,1)} %collective-permute-done.7.rest1), channel_id=1, source_target_pairs={{0,4},{1,5},{2,6},{3,7},{4,8},{5,9},{6,10},{7,11},{8,12},{9,13},{1... | collective-permute-start | bytes 1179656 | tf_op jit(solution)/shard_map/ppermute | solution.py:519
  51.0 30.4 %collective-permute-start.12 = (bf16[256,1024]{1,0:T(8,128)(2,1)}, bf16[256,1024]{1,0:T(8,128)(2,1)S(1)}, u32[]{:S(2)}, u32[]{:S(2)}) collective-permute-start(bf16[256,1024]{1,0:T(8,128)(2,1)} %collective-permute-done.11), channel_id=1, source_target_pairs={{0,1},{1,0},{2,3},{3,2},{4,5},{5,4},{6,7},{7,6},{8,9},{9,8},{10,11... | collective-permute-start | bytes 1572872 | tf_op jit(solution)/shard_map/ppermute | solution.py:514
  51.6 1.0 copy-start.8
  52.6 0.7 copy-start.10
  53.3 0.7 copy-start.12
  54.0 11.3 %copy-start.4 = (bf16[1024,1024]{1,0:T(8,128)(2,1)S(1)}, bf16[1024,1024]{1,0:T(8,128)(2,1)}, u32[]{:S(2)}) copy-start(bf16[1024,1024]{1,0:T(8,128)(2,1)} %constant_dynamic-update-slice_fusion.6) | copy-start | bytes 6291460
  65.2 4.9 %copy-start.9 = (bf16[1040,128]{1,0:T(8,128)(2,1)S(1)}, bf16[1040,128]{1,0:T(8,128)(2,1)}, u32[]{:S(2)}) copy-start(bf16[1040,128]{1,0:T(8,128)(2,1)} %copy-done.7) | copy-start | bytes 798724
  67.4 14.0 %copy-start.14 = (bf16[4,1,64,1024]{3,2,1,0:T(8,128)(2,1)S(1)}, bf16[4,1,64,1024]{3,2,1,0:T(8,128)(2,1)}, u32[]{:S(2)}) copy-start(bf16[4,1,64,1024]{3,2,1,0:T(8,128)(2,1)} %constant_dynamic-slice_fusion) | copy-start | bytes 1572868
  67.5 32.9 %collective-permute-start.17 = (bf16[1536,128]{1,0:T(8,128)(2,1)S(1)}, bf16[1536,128]{1,0:T(8,128)(2,1)S(1)}, u32[]{:S(2)}, u32[]{:S(2)}) collective-permute-start(bf16[1536,128]{1,0:T(8,128)(2,1)S(1)} %collective-permute-done.16.rest1), channel_id=1, source_target_pairs={{0,4},{1,5},{2,6},{3,7},{4,8},{5,9},{6,10},{7,11},{8,12},{9,13},{1... | collective-permute-start | bytes 1179656 | tf_op jit(solution)/shard_map/ppermute | solution.py:519
  81.5 0.9 copy-start.6
  81.5 0.9 copy-start.11
  81.5 0.9 copy-start.13
  95.3 40.9 %collective-permute-start.13 = (bf16[768,128]{1,0:T(8,128)(2,1)S(1)}, bf16[768,128]{1,0:T(8,128)(2,1)S(1)}, u32[]{:S(2)}, u32[]{:S(2)}) collective-permute-start(bf16[768,128]{1,0:T(8,128)(2,1)S(1)} %get-tuple-element.56), channel_id=1, source_target_pairs={{0,1},{1,0},{2,3},{3,2},{4,5},{5,4},{6,7},{7,6},{8,9},{9,8},{10,11... | collective-permute-start | bytes 589832 | tf_op jit(solution)/shard_map/ppermute | solution.py:514
  95.9 15.8 %collective-permute-start.23 = (bf16[64,1024]{1,0:T(8,128)(2,1)S(1)}, bf16[64,1024]{1,0:T(8,128)(2,1)S(1)}, u32[]{:S(2)}, u32[]{:S(2)}) collective-permute-start(bf16[64,1024]{1,0:T(8,128)(2,1)S(1)} %get-tuple-element.73), channel_id=1, source_target_pairs={{4,0},{5,1},{6,2},{7,3},{8,4},{9,5},{10,6},{11,7},{20,16},{21,17},... | collective-permute-start | bytes 393224 | tf_op jit(solution)/shard_map/ppermute | solution.py:576
  97.8 21.9 %collective-permute-start.22 = (bf16[64,1024]{1,0:T(8,128)(2,1)S(1)}, bf16[64,1024]{1,0:T(8,128)(2,1)S(1)}, u32[]{:S(2)}, u32[]{:S(2)}) collective-permute-start(bf16[64,1024]{1,0:T(8,128)(2,1)S(1)} %get-tuple-element.72), channel_id=1, source_target_pairs={{8,0},{9,1},{10,2},{11,3},{12,4},{13,5},{14,6},{15,7},{24,16},{25,... | collective-permute-start | bytes 393224 | tf_op jit(solution)/shard_map/ppermute | solution.py:576
  99.1 32.3 %collective-permute-start.21 = (bf16[64,1024]{1,0:T(8,128)(2,1)S(1)}, bf16[64,1024]{1,0:T(8,128)(2,1)S(1)}, u32[]{:S(2)}, u32[]{:S(2)}) collective-permute-start(bf16[64,1024]{1,0:T(8,128)(2,1)S(1)} %get-tuple-element.71), channel_id=1, source_target_pairs={{0,4},{1,5},{2,6},{3,7},{12,0},{13,1},{14,2},{15,3},{16,20},{17,21... | collective-permute-start | bytes 393224 | tf_op jit(solution)/shard_map/ppermute | solution.py:576
  103.3 30.4 %collective-permute-start.26 = (bf16[64,1024]{1,0:T(8,128)(2,1)S(1)}, bf16[64,1024]{1,0:T(8,128)(2,1)S(1)}, u32[]{:S(2)}, u32[]{:S(2)}) collective-permute-start(bf16[64,1024]{1,0:T(8,128)(2,1)S(1)} %get-tuple-element.77), channel_id=1, source_target_pairs={{0,12},{1,13},{2,14},{3,15},{12,8},{13,9},{14,10},{15,11},{16,28},... | collective-permute-start | bytes 393224 | tf_op jit(solution)/shard_map/ppermute | solution.py:576
  111.7 22.8 %collective-permute-start.25 = (bf16[64,1024]{1,0:T(8,128)(2,1)S(1)}, bf16[64,1024]{1,0:T(8,128)(2,1)S(1)}, u32[]{:S(2)}, u32[]{:S(2)}) collective-permute-start(bf16[64,1024]{1,0:T(8,128)(2,1)S(1)} %get-tuple-element.76), channel_id=1, source_target_pairs={{0,8},{1,9},{2,10},{3,11},{4,12},{5,13},{6,14},{7,15},{16,24},{17,... | collective-permute-start | bytes 393224 | tf_op jit(solution)/shard_map/ppermute | solution.py:576
  119.7 15.1 %collective-permute-start.24 = (bf16[64,1024]{1,0:T(8,128)(2,1)S(1)}, bf16[64,1024]{1,0:T(8,128)(2,1)S(1)}, u32[]{:S(2)}, u32[]{:S(2)}) collective-permute-start(bf16[64,1024]{1,0:T(8,128)(2,1)S(1)} %get-tuple-element.75), channel_id=1, source_target_pairs={{4,8},{5,9},{6,10},{7,11},{8,12},{9,13},{10,14},{11,15},{20,24},{2... | collective-permute-start | bytes 393224 | tf_op jit(solution)/shard_map/ppermute | solution.py:576
  131.4 6.8 %collective-permute-start.14 = (bf16[768,128]{1,0:T(8,128)(2,1)S(1)}, bf16[768,128]{1,0:T(8,128)(2,1)S(1)}, u32[]{:S(2)}, u32[]{:S(2)}) collective-permute-start(bf16[768,128]{1,0:T(8,128)(2,1)S(1)} %get-tuple-element.57), channel_id=1, source_target_pairs={{0,2},{1,3},{2,0},{3,1},{4,6},{5,7},{6,4},{7,5},{8,10},{9,11},{10,... | collective-permute-start | bytes 589832 | tf_op jit(solution)/shard_map/ppermute | solution.py:514
  133.7 10.4 %collective-permute-start.15 = (bf16[768,128]{1,0:T(8,128)(2,1)S(1)}, bf16[768,128]{1,0:T(8,128)(2,1)S(1)}, u32[]{:S(2)}, u32[]{:S(2)}) collective-permute-start(bf16[768,128]{1,0:T(8,128)(2,1)S(1)} %get-tuple-element.58), channel_id=1, source_target_pairs={{0,3},{1,2},{2,1},{3,0},{4,7},{5,6},{6,5},{7,4},{8,11},{9,10},{10,... | collective-permute-start | bytes 589832 | tf_op jit(solution)/shard_map/ppermute | solution.py:514
  134.5 9.6 %collective-permute-start.18 = (bf16[768,128]{1,0:T(8,128)(2,1)S(1)}, bf16[768,128]{1,0:T(8,128)(2,1)S(1)}, u32[]{:S(2)}, u32[]{:S(2)}) collective-permute-start(bf16[768,128]{1,0:T(8,128)(2,1)S(1)} %get-tuple-element.64), channel_id=1, source_target_pairs={{0,1},{1,0},{2,3},{3,2},{4,5},{5,4},{6,7},{7,6},{8,9},{9,8},{10,11... | collective-permute-start | bytes 589832 | tf_op jit(solution)/shard_map/ppermute | solution.py:514
  134.9 11.7 %collective-permute-start.19 = (bf16[768,128]{1,0:T(8,128)(2,1)S(1)}, bf16[768,128]{1,0:T(8,128)(2,1)S(1)}, u32[]{:S(2)}, u32[]{:S(2)}) collective-permute-start(bf16[768,128]{1,0:T(8,128)(2,1)S(1)} %get-tuple-element.65), channel_id=1, source_target_pairs={{0,2},{1,3},{2,0},{3,1},{4,6},{5,7},{6,4},{7,5},{8,10},{9,11},{10,... | collective-permute-start | bytes 589832 | tf_op jit(solution)/shard_map/ppermute | solution.py:514
  136.2 15.3 %collective-permute-start.20 = (bf16[768,128]{1,0:T(8,128)(2,1)S(1)}, bf16[768,128]{1,0:T(8,128)(2,1)S(1)}, u32[]{:S(2)}, u32[]{:S(2)}) collective-permute-start(bf16[768,128]{1,0:T(8,128)(2,1)S(1)} %get-tuple-element.66), channel_id=1, source_target_pairs={{0,3},{1,2},{2,1},{3,0},{4,7},{5,6},{6,5},{7,4},{8,11},{9,10},{10,... | collective-permute-start | bytes 589832 | tf_op jit(solution)/shard_map/ppermute | solution.py:514

commit v2 on v1

--- a/solution.py
+++ b/solution.py
@@ -14,7 +14,8 @@
 LANES = 128
 NEG = -1e30
 PAD = 3e30
-VMEM_LIMIT = 48 * 1024 * 1024
+VMEM_LIMIT = 16 * 1024 * 1024
+SMALL = pl.CostEstimate(flops=1_000_000, bytes_accessed=100_000, transcendentals=0)
 
 F32 = jnp.float32
 BF16 = jnp.bfloat16
@@ -44,56 +45,138 @@
     return even, odd
 
 
-def pack_kernel(me_ref, q_ref, k_ref, v_ref, t_ref, own_ref, *outs):
-    first, second = outs[:ROW], outs[ROW:]
+def packed(me_ref, src, chunk, pair):
     r = me_ref[0]
     odd_me = (r % 2) == 1
-    rows = q_ref.shape[0]
+    tile = 4 * chunk + (r // 2 + pair) % 2
+    a = src[:, pl.ds(pl.multiple_of(tile * LANES, LANES), LANES)].astype(F32)
+    b = src[:, pl.ds(pl.multiple_of((tile + 2) * LANES, LANES), LANES)].astype(F32)
+    even, odd = split_pair(a, b)
+    return jnp.where(odd_me, odd, even), jnp.where(odd_me, even, odd)
+
+
+def pack_first_kernel(me_ref, k_ref, v_ref, own_ref, *outs):
+    rows = k_ref.shape[0]
+    for which, src in enumerate((k_ref, v_ref)):
+        for side, value in enumerate(packed(me_ref, src, 1, 0)):
+            if side == 0:
+                base = (2 + which) * rows
+                own_ref[base : base + rows, :] = value.astype(BF16)
+        for pair in (0, 1):
+            for side, value in enumerate(packed(me_ref, src, 0, pair)):
+                d = 2 * pair + side
+                value = value.astype(BF16)
+                base = which * rows
+                if d == 0:
+                    own_ref[base : base + rows, :] = value
+                else:
+                    outs[d - 1][base : base + rows, :] = value
+
+
+def pack_second_kernel(me_ref, q_ref, k_ref, v_ref, t_ref, *outs):
+    rows = k_ref.shape[0]
     per = rows // BLOCK
-
-    def pieces(src, chunk, pair):
-        tile = 4 * chunk + (r // 2 + pair) % 2
-        a = src[:, pl.ds(pl.multiple_of(tile * LANES, LANES), LANES)].astype(F32)
-        b = src[:, pl.ds(pl.multiple_of((tile + 2) * LANES, LANES), LANES)].astype(F32)
-        even, odd = split_pair(a, b)
-        return jnp.where(odd_me, odd, even), jnp.where(odd_me, even, odd)
-
-    for chunk in (0, 1):
-        for pair in (0, 1):
-            for which, src in enumerate((k_ref, v_ref)):
-                for side, value in enumerate(pieces(src, chunk, pair)):
-                    value = value.astype(BF16)
-                    d = 2 * pair + side
-                    target = (first, second)[chunk][d]
-                    target[which * rows : (which + 1) * rows, :] = value
-                    if d == 0:
-                        base = (2 * chunk + which) * rows
-                        own_ref[base : base + rows, :] = value
-            for side, value in enumerate(pieces(q_ref, chunk, pair)):
-                d = 2 * pair + side
+    for pair in (0, 1):
+        for which, src in enumerate((k_ref, v_ref)):
+            for side, value in enumerate(packed(me_ref, src, 1, pair)):
+                outs[2 * pair + side][which * rows : (which + 1) * rows, :] = value.astype(BF16)
+        for chunk in (0, 1):
+            for side, value in enumerate(packed(me_ref, q_ref, chunk, pair)):
                 scaled = value * 0.125
                 for b in range(per):
                     base = 2 * rows + (chunk * per + b) * LANES
                     turned = scaled[b * BLOCK : (b + 1) * BLOCK].T
-                    second[d][base : base + LANES, :] = turned.astype(BF16)
+                    outs[2 * pair + side][base : base + LANES, :] = turned.astype(BF16)
+    for out in outs:
+        out[4 * rows : 4 * rows + 16, :] = t_ref[...]
+
+
+def pack_first(me, keys, values):
+    rows = keys.shape[0]
+    outs = pl.pallas_call(
+        pack_first_kernel,
+        out_shape=(jax.ShapeDtypeStruct((4 * rows, LANES), BF16),)
+        + (jax.ShapeDtypeStruct((2 * rows, LANES), BF16),) * 3,
+        in_specs=[SMEM] + [VMEM] * 2,
+        out_specs=[VMEM] * 4,
+        compiler_params=params(),
+        cost_estimate=SMALL,
+        name="pack_first",
+    )(me, keys, values)
+    return outs[0], outs[1:]
+
+
+def pack_second(me, queries, keys, values, track_block):
+    rows = queries.shape[0]
+    return pl.pallas_call(
+        pack_second_kernel,
+        out_shape=(jax.ShapeDtypeStruct((4 * rows + 16, LANES), BF16),) * ROW,
+        in_specs=[SMEM] + [VMEM] * 4,
+        out_specs=[VMEM] * ROW,
+        compiler_params=params(),
+        cost_estimate=SMALL,
+        name="pack_second",
+    )(me, queries, keys, values, track_block)
+
+
+def stack_kernel(rows, a, b, c, out):
+    for i, src in enumerate((a, b, c)):
+        out[i * rows : (i + 1) * rows, :] = src[0:rows, :]
+
+
+def stack(rows, pieces):
+    return pl.pallas_call(
+        functools.partial(stack_kernel, rows),
+        out_shape=jax.ShapeDtypeStruct((3 * rows, LANES), BF16),
+        in_specs=[VMEM] * 3,
+        out_specs=VMEM,
+        compiler_params=params(),
+        cost_estimate=SMALL,
+        name="stack",
+    )(*pieces)
+
+
+def grad_kernel(me_ref, w, g0, g1, g2, g3, out, wide_w, wide_g, sem):
+    r = me_ref[0]
+    half = LANES // 2
+    rows = g0.shape[0]
+    copies = [
+        pltpu.make_async_copy(
+            w.at[pl.ds(pl.multiple_of((ROW * j + r) * half, half), half)],
+            wide_w.at[pl.ds(j * half, half)],
+            sem.at[j],
+        )
+        for j in range(ROW)
+    ]
+    copies += [
+        pltpu.make_async_copy(g, wide_g.at[pl.ds(d * rows, rows)], sem.at[ROW + d])
+        for d, g in enumerate((g0, g1, g2, g3))
+    ]
+    for copy in copies:
+        copy.start()
+    for copy in copies:
+        copy.wait()
     for d in range(ROW):
-        second[d][4 * rows : 4 * rows + 16, :] = t_ref[...]
-
-
-def pack(me, queries, keys, values, track_block):
-    rows = queries.shape[0]
-    one = jax.ShapeDtypeStruct((2 * rows, LANES), BF16)
-    two = jax.ShapeDtypeStruct((4 * rows + 16, LANES), BF16)
-    own = jax.ShapeDtypeStruct((4 * rows, LANES), BF16)
-    outs = pl.pallas_call(
-        pack_kernel,
-        out_shape=(own,) + (one,) * ROW + (two,) * ROW,
-        in_specs=[SMEM] + [VMEM] * 4,
-        out_specs=[VMEM] * 9,
-        compiler_params=params(),
-        name="pack",
-    )(me, queries, keys, values, track_block)
-    return outs[0], outs[1:5], outs[5:]
+        piece = wide_g[d * rows : (d + 1) * rows, :]
+        out[:, d * rows : (d + 1) * rows] = nt(wide_w[...], piece).astype(BF16)
+
+
+def grad_turned(me, weight, gos):
+    rows, width = gos[0].shape
+    return pl.pallas_call(
+        grad_kernel,
+        out_shape=jax.ShapeDtypeStruct((2 * LANES, ROW * rows), BF16),
+        in_specs=[SMEM] + [ANY] * 5,
+        out_specs=VMEM,
+        scratch_shapes=[
+            pltpu.VMEM((2 * LANES, width), BF16),
+            pltpu.VMEM((ROW * rows, width), BF16),
+            pltpu.SemaphoreType.DMA((2 * ROW,)),
+        ],
+        compiler_params=params(),
+        cost_estimate=SMALL,
+        name="grad_attn",
+    )(me, weight, *gos)
 
 
 def plan_kernel(me_ref, track_ref, list_ref, count_ref):
@@ -105,29 +188,15 @@
         rho = r ^ d
         span = ROW * z + rho
 
-        def clear(i, c):
-            list_ref[qi, i] = 0
-            return c
-
-        lax.fori_loop(0, 24, clear, 0)
-
-        def step(i, state):
-            near, total = state
+        near, total = jnp.int32(0), jnp.int32(0)
+        for i in range(2 * WINDOW):
             u = span - (i // 2 + 1)
-            use = jnp.logical_and(track_ref[qi, i] == 1, u >= 0)
+            use = jnp.logical_and(track_ref[qi, i] == 1, u >= 0).astype(jnp.int32)
             safe = jnp.maximum(u, 0)
             back = z - safe // ROW
-            slot = ((back * ROW + (r ^ (safe % ROW))) * 4) + i % 2
-
-            @pl.when(use)
-            def _():
-                list_ref[qi, total] = slot
-
-            use = use.astype(jnp.int32)
+            list_ref[qi, total] = ((back * ROW + (r ^ (safe % ROW))) * 4) + i % 2
             near = near + jnp.where(back < 2, use, 0)
-            return near, total + use
-
-        near, total = lax.fori_loop(0, 2 * WINDOW, step, (0, 0))
+            total = total + use
         count_ref[qi, 0] = near
         count_ref[qi, 1] = total
         return carry
@@ -144,6 +213,7 @@
         ),
         in_specs=[SMEM, SMEM],
         out_specs=[SMEM, SMEM],
+        cost_estimate=SMALL,
         name="plan",
     )(me, track_row)
 
@@ -227,7 +297,7 @@
 
 
 def near_kernel(
-    chunk, list_ref, count_ref, own0, rest0, own1, rest1, s0, s1, s2, s3, m_ref, acc_ref, kv, vt, qt, sem
+    chunk, list_ref, count_ref, own0, rest0, own1, rest1, s0, s1, s2, s3, after, m_ref, acc_ref, kv, vt, qt, sem
 ):
     copies = row_copies(chunk, 256, 0, own0, rest0, kv, sem, 0)
     copies += row_copies(chunk, 256, 1, own1, rest1, kv, sem, 2)
@@ -261,14 +331,14 @@
         lax.fori_loop(0, (longest + 1) // 4, body, 0)
 
 
-def near(chunk, lists, counts, own0, rest0, own1, rest1, seconds):
+def near(chunk, lists, counts, own0, rest0, own1, rest1, seconds, after):
     return pl.pallas_call(
         functools.partial(near_kernel, chunk),
         out_shape=(
             jax.ShapeDtypeStruct((8, 8, 256), F32),
             jax.ShapeDtypeStruct((8, 144, 256), F32),
         ),
-        in_specs=[SMEM, SMEM] + [ANY] * 8,
+        in_specs=[SMEM, SMEM] + [ANY] * 9,
         out_specs=[VMEM, VMEM],
         scratch_shapes=[
             pltpu.VMEM((32, BLOCK, LANES), BF16),
@@ -277,26 +347,30 @@
             pltpu.SemaphoreType.DMA((8,)),
         ],
         compiler_params=params(),
-        cost_estimate=pl.CostEstimate(flops=8_000_000_000, bytes_accessed=4_000_000, transcendentals=0),
+        cost_estimate=SMALL,
         name=f"near{chunk}",
-    )(lists, counts, own0, rest0, own1, rest1, *seconds)
+    )(lists, counts, own0, rest0, own1, rest1, *seconds, after)
 
 
 def far_kernel(
-    chunk, fast, me_ref, list_ref, count_ref, own2, rest2, s0, s1, s2, s3, go, m_in, acc_in, *refs
+    chunk, last, me_ref, list_ref, count_ref, own2, rest2, s0, s1, s2, s3, g0, g1, g2, g3,
+    m_in, acc_in, after, earlier, attn_ref, lse_ref, *refs
 ):
-    if fast:
-        attn_ref, lse_ref, w0, w1, w2, w3, m_ref, acc_ref, kv, vt, qt, go_v, wide, sem = refs
-    else:
-        attn_ref, lse_ref, w0, m_ref, acc_ref, kv, vt, qt, go_v, wide, sem = refs
+    *terms, m_ref, acc_ref, kv, vt, qt, go_v, wide, sem = refs
     copies = row_copies(chunk, 256, 0, own2, rest2, kv, sem, 0)
     copies += query_copies(chunk, (s0, s1, s2, s3), qt, sem, 2)
     copies.append(pltpu.make_async_copy(m_in, m_ref, sem.at[6]))
     copies.append(pltpu.make_async_copy(acc_in, acc_ref, sem.at[7]))
-    go_copy = pltpu.make_async_copy(go, go_v, sem.at[8])
+    late = [
+        pltpu.make_async_copy(g, go_v.at[pl.ds(d * 256, 256)], sem.at[8 + d])
+        for d, g in enumerate((g0, g1, g2, g3))
+    ]
+    if last:
+        late.append(pltpu.make_async_copy(earlier, wide.at[pl.ds(0, LANES)], sem.at[12]))
     for copy in copies:
         copy.start()
-    go_copy.start()
+    for copy in late:
+        copy.start()
     for copy in copies:
         copy.wait()
     base = 8 * ROW
@@ -321,36 +395,35 @@
         lse_ref[qi] = m_ref[qi] + jnp.log(jnp.broadcast_to(total, m_ref.shape[1:]))
         out = pick_heads(acc_ref[qi, 0:LANES, :] / total)
         attn_ref[:, qi * BLOCK : (qi + 1) * BLOCK] = out.astype(BF16)
-    go_copy.wait()
-    wide[...] = nn(attn_ref[...], go_v[...])
-    if fast:
-        z = me_ref[1]
-        half = LANES // 2
-        for delta, w in enumerate((w0, w1, w2, w3)):
-            target = (z + delta) % 4 - 2 * chunk
-            inside = jnp.logical_and(target >= 0, target < 2)
-            at = pl.multiple_of(jnp.where(inside, target, 0) * half, half)
-            piece = wide[pl.ds(at, half), :]
-            w[...] = jnp.where(inside, piece, 0.0).astype(BF16)
-    else:
-        w0[...] = wide[...].astype(BF16)
-
-
-def far(chunk, fast, me, lists, counts, own2, rest2, seconds, go, m, acc):
-    width = go.shape[1]
+    for copy in late:
+        copy.wait()
+    term = nn(attn_ref[...], go_v[...])
+    if not last:
+        terms[0][...] = term.astype(BF16)
+        return
+    wide[LANES : 2 * LANES, :] = term.astype(BF16)
+    z = me_ref[1]
+    half = LANES // 2
+    for delta, out in enumerate(terms):
+        at = pl.multiple_of((z + delta) % ROW * half, half)
+        out[...] = wide[pl.ds(at, half), :]
+
+
+def far(chunk, last, me, lists, counts, own2, rest2, seconds, gos, m, acc, after, earlier):
+    width = gos[0].shape[1]
     weights = (
         (jax.ShapeDtypeStruct((LANES // 2, width), BF16),) * 4
-        if fast
+        if last
         else (jax.ShapeDtypeStruct((LANES, width), BF16),)
     )
     return pl.pallas_call(
-        functools.partial(far_kernel, chunk, fast),
+        functools.partial(far_kernel, chunk, last),
         out_shape=(
             jax.ShapeDtypeStruct((LANES, 8 * BLOCK), BF16),
             jax.ShapeDtypeStruct((8, 8, 256), F32),
         )
         + weights,
-        in_specs=[SMEM, SMEM, SMEM] + [ANY] * 9,
+        in_specs=[SMEM, SMEM, SMEM] + [ANY] * 14,
         out_specs=[VMEM] * (2 + len(weights)),
         scratch_shapes=[
             pltpu.VMEM((8, 8, 256), F32),
@@ -358,14 +431,14 @@
             pltpu.VMEM((16, BLOCK, LANES), BF16),
             pltpu.VMEM((16, 144, LANES), BF16),
             pltpu.VMEM((8, LANES, BLOCK), BF16),
-            pltpu.VMEM(go.shape, BF16),
-            pltpu.VMEM((LANES, width), F32),
-            pltpu.SemaphoreType.DMA((9,)),
+            pltpu.VMEM((ROW * gos[0].shape[0], width), BF16),
+            pltpu.VMEM((2 * LANES, width), BF16),
+            pltpu.SemaphoreType.DMA((13,)),
         ],
         compiler_params=params(),
-        cost_estimate=pl.CostEstimate(flops=5_000_000_000, bytes_accessed=6_000_000, transcendentals=0),
+        cost_estimate=SMALL,
         name=f"far{chunk}",
-    )(me, lists, counts, own2, rest2, *seconds, go, m, acc)
+    )(me, lists, counts, own2, rest2, *seconds, *gos, m, acc, after, earlier)
 
 
 def bwd_group(kv, kt, q2, g2, lse, delta, fs, pads, diag=None):
@@ -473,7 +546,7 @@
             pltpu.SemaphoreType.DMA((10,)),
         ],
         compiler_params=params(),
-        cost_estimate=pl.CostEstimate(flops=10_000_000_000, bytes_accessed=8_000_000, transcendentals=0),
+        cost_estimate=SMALL,
         name=f"back{chunk}",
     )(lists, counts, *row0, *row1, *row2, *seconds, gt, attn, lse)
 
@@ -505,6 +578,7 @@
         in_specs=[SMEM] + [VMEM] * 8,
         out_specs=[VMEM] * 3,
         compiler_params=params(),
+        cost_estimate=SMALL,
         name="unpack",
     )(me, *pieces)
 
@@ -517,6 +591,9 @@
 def later(value, axis):
     count = lax.axis_size(axis)
     return lax.ppermute(value, axis, [(s, s + ROW) for s in range(count - ROW)])
+
+
+hold = lax.optimization_barrier
 
 
 def shards(queries, keys, values, track, out_weight, grad_out):
@@ -527,56 +604,54 @@
     me = jnp.stack([r, z])
     fast = count == HEADS
     track_block = jnp.pad(track.astype(BF16), ((0, 14), (0, LANES - track.shape[1])))
-    own0, firsts, seconds = pack(me, queries, keys, values, track_block)
-
+
+    own0, firsts = pack_first(me, keys, values)
     own1 = later(own0, "span")
-    got_first = [swap(firsts[d], "span", d) for d in (1, 2, 3)]
-    got_second = [swap(seconds[d], "span", d) for d in (1, 2, 3)]
+    got_first = [swap(x, "span", d + 1) for d, x in enumerate(firsts)]
+    rest0 = [stack(2 * rows, got_first)]
+    rest1 = [later(rest0[0], "span")]
+
+    queries, _ = hold((queries, got_first[0]))
+    seconds = list(pack_second(me, queries, keys, values, track_block))
+    seconds, _ = hold((seconds, (rest0[0], own1)))
+    seconds[1:] = [swap(seconds[d], "span", d) for d in (1, 2, 3)]
     own2 = later(own1, "span")
-    seconds = [seconds[0]] + got_second
-    rest0 = [
-        jnp.concatenate(got_first, axis=0),
-        jnp.concatenate([x[: 2 * rows] for x in got_second], axis=0),
-    ]
-    rest1 = [later(x, "span") for x in rest0]
-    rest2 = [later(x, "span") for x in rest1]
-
-    go2 = swap(grad_out, "span", 2)
-    go1 = swap(grad_out, "span", 1)
-    go3 = swap(go2, "span", 1)
-    go = jnp.concatenate([grad_out, go1, go2, go3], axis=0)
-
     track_row = jnp.concatenate([x[4 * rows : 4 * rows + 2, : 2 * WINDOW] for x in seconds], axis=0)
     lists, counts = plan(me, track_row.astype(jnp.int32))
-
-    head_dim = width // HEADS
-    weight_rows = lax.dynamic_index_in_dim(
-        out_weight.reshape(ROW, ROW, head_dim, width), r, 1, keepdims=False
-    ).reshape(ROW * head_dim, width)
-    grad_turned = lax.dot_general(
-        weight_rows, go, (((1,), (1,)), ((), ())), preferred_element_type=F32
-    ).astype(BF16)
-
-    states, pieces, weights = [], [], []
+    arrived, _ = hold((seconds[1:], (rest1[0], own2, lists)))
+    rest0.append(stack(2 * rows, arrived))
+    rest1.append(later(rest0[1], "span"))
+    rest2 = [later(x, "span") for x in rest1]
+    grad_late, _ = hold((grad_out, rest0[1]))
+    go2 = swap(grad_late, "span", 2)
+
+    states, pieces = [], []
+    after = lists
     for chunk in (0, 1):
-        states.append(near(chunk, lists, counts, own0, rest0[chunk], own1, rest1[chunk], seconds))
+        states.append(near(chunk, lists, counts, own0, rest0[chunk], own1, rest1[chunk], seconds, after))
+        after = states[-1][0]
+        if chunk == 0:
+            (grad_late, go2), _ = hold(((grad_out, go2), after))
+            gos = (grad_out, swap(grad_late, "span", 1), go2, swap(go2, "span", 1))
+            grads = grad_turned(me, out_weight, gos)
+    terms = [after]
     for chunk in (0, 1):
+        last = chunk == 1 and fast
         attn, lse, *terms = far(
-            chunk, fast, me, lists, counts, own2, rest2[chunk], seconds, go, *states[chunk]
+            chunk, last, me, lists, counts, own2, rest2[chunk], seconds, gos, *states[chunk],
+            after, terms[0],
         )
-        if fast:
-            received = [terms[0].astype(F32)]
+        if last:
+            weight_grad = terms[0].astype(F32)
             for delta in (1, 2, 3):
                 pairs = [
                     (ROW * s + q, ROW * ((s + delta) % ROW) + q)
                     for s in range(ROW)
                     for q in range(ROW)
-                    if (s + delta) % ROW // 2 == chunk
                 ]
-                received.append(lax.ppermute(terms[delta], "span", pairs).astype(F32))
-            weights += received
-        else:
-            weights.append(terms[0])
+                weight_grad += lax.ppermute(terms[delta], "span", pairs).astype(F32)
+        elif not fast:
+            pieces_w = [terms[0]] if chunk == 0 else [pieces_w[0], terms[0]]
         out = back(
             chunk,
             lists,
@@ -585,17 +660,19 @@
             (own1, rest1[chunk]),
             (own2, rest2[chunk]),
             seconds,
-            grad_turned[chunk * LANES : (chunk + 1) * LANES],
+            grads[chunk * LANES : (chunk + 1) * LANES],
             attn,
             lse,
         )
-        pieces.append(out[0])
+        after = out[0]
+        if chunk == 1:
+            out, pieces = hold((out, pieces))
+        pieces = list(pieces) + [out[0]]
         pieces += [swap(out[d], "span", d) for d in (1, 2, 3)]
     query_grad, key_grad, value_grad = unpack(me, pieces, rows, width)
-    if fast:
-        weight_grad = functools.reduce(lambda a, b: a + b, weights)
-    else:
-        mine = jnp.concatenate(weights, axis=0).reshape(ROW, 1, head_dim, width)
+    if not fast:
+        head_dim = width // HEADS
+        mine = jnp.concatenate(pieces_w, axis=0).reshape(ROW, 1, head_dim, width)
         full = jnp.zeros((ROW, ROW, head_dim, width), BF16)
         full = lax.dynamic_update_slice(full, mine, (0, r, 0, 0)).reshape(width, width)
         weight_grad = lax.psum_scatter(full.astype(F32), "span", scatter_dimension=0, tiled=True)

time: 156 us -> 139 us (0.89)
  the two profiles are of different devices: /device:TPU:11 before, /device:TPU:13 now
where the time goes in v2:
time: 139 us; the launch traced here: 138 us
  Pallas kernels  60.7 us (44%)
  starting transfers between devices  38.4 us (28%)
  waiting for transfers between devices  33.9 us (24%)
  local copies, waits for them, and re-layouts  2.5 us (2%)
  other arithmetic  1.46 us (1%)
    ppermute x15, waiting for transfers between devices, swap(): return lax.ppermute(value, axis, [(s, s ^ bit) for s in range(count)])  25.9 us
    pallas_call x2, Pallas kernels, near(): pl.pallas_call(functools.partial(near_kernel, chunk), out_shape=(jax.Shap...  23.7 us
    pallas_call x2, Pallas kernels, back(): pl.pallas_call(functools.partial(back_kernel, chunk), out_shape=(jax.Shap...  21.9 us
    ppermute x6, starting transfers between devices, later(): return lax.ppermute(value, axis, [(s, s + ROW) for s in range(count - ROW)])  14.5 us
    ppermute x15, starting transfers between devices, swap(): return lax.ppermute(value, axis, [(s, s ^ bit) for s in range(count)])  13.4 us
    ppermute x3, starting transfers between devices, shards(): weight_grad += lax.ppermute(terms[delta], 'span', pairs).astype(F32)  10.5 us
    ppermute x6, waiting for transfers between devices, later(): return lax.ppermute(value, axis, [(s, s + ROW) for s in range(count - ROW)])  8.01 us
    pallas_call x2, Pallas kernels, far(): pl.pallas_call(functools.partial(far_kernel, chunk, last), out_shape=(jax...  5.91 us
  transfers between devices with their start and end apart: 24, of which 8 were waited for; matrix products, arithmetic and copies ran while one was open for 1% of the time, Pallas kernels for 42%

profile of v2, /device:TPU:13, one launch (start us, length us, event | category | flops | bytes accessed | tf_op | source)
XLA Modules:
  0.0 137.9 jit_solution(2834213889626312807)
XLA Ops:
  0.7 0.1 pad_add_fusion.me_ref
  0.7 1.0 copy-done.2
  1.8 1.0 copy-done.4
  2.8 1.0 pack_first.1
  3.8 3.2 %collective-permute-start.3 = (bf16[1024,128]{1,0:T(8,128)(2,1)S(1)}, bf16[1024,128]{1,0:T(8,128)(2,1)S(1)}, u32[]{:S(2)}, u32[]{:S(2)}) collective-permute-start(bf16[1024,128]{1,0:T(8,128)(2,1)S(1)} %get-tuple-element.65.own0), channel_id=1, source_target_pairs={{0,4},{1,5},{2,6},{3,7},{4,8},{5,9},{6,10},{7,11},{8,12},{9,13},{1... | collective-permute-start | bytes 786440 | tf_op jit(solution)/shard_map/ppermute | solution.py:593
  7.0 1.0 collective-permute-start
  8.0 0.2 collective-permute-start.1
  8.3 1.5 %collective-permute-start.2 = (bf16[512,128]{1,0:T(8,128)(2,1)S(1)}, bf16[512,128]{1,0:T(8,128)(2,1)S(1)}, u32[]{:S(2)}, u32[]{:S(2)}) collective-permute-start(bf16[512,128]{1,0:T(8,128)(2,1)S(1)} %get-tuple-element.64), channel_id=1, source_target_pairs={{0,3},{1,2},{2,1},{3,0},{4,7},{5,6},{6,5},{7,4},{8,11},{9,10},{10,... | collective-permute-start | bytes 393224 | tf_op jit(solution)/shard_map/ppermute | solution.py:588
  9.7 0.0 collective-permute-done.a
  9.7 3.4 %collective-permute-done.1.b = bf16[512,128]{1,0:T(8,128)(2,1)S(1)} collective-permute-done((bf16[512,128]{1,0:T(8,128)(2,1)S(1)}, bf16[512,128]{1,0:T(8,128)(2,1)S(1)}, u32[]{:S(2)}, u32[]{:S(2)}) %collective-permute-start.1) | collective-permute-done | bytes 131104 | tf_op jit(solution)/shard_map/ppermute | solution.py:588
  13.1 3.0 %collective-permute-done.2.c = bf16[512,128]{1,0:T(8,128)(2,1)S(1)} collective-permute-done((bf16[512,128]{1,0:T(8,128)(2,1)S(1)}, bf16[512,128]{1,0:T(8,128)(2,1)S(1)}, u32[]{:S(2)}, u32[]{:S(2)}) %collective-permute-start.2) | collective-permute-done | bytes 131104 | tf_op jit(solution)/shard_map/ppermute | solution.py:588
  16.1 3.2 %collective-permute-start.7 = (bf16[1536,128]{1,0:T(8,128)(2,1)S(1)}, bf16[1536,128]{1,0:T(8,128)(2,1)S(1)}, u32[]{:S(2)}, u32[]{:S(2)}) collective-permute-start(bf16[1536,128]{1,0:T(8,128)(2,1)S(1)} %stack.14.rest0), channel_id=1, source_target_pairs={{0,4},{1,5},{2,6},{3,7},{4,8},{5,9},{6,10},{7,11},{8,12},{9,13},{1... | collective-permute-start | bytes 1179656 | tf_op jit(solution)/shard_map/ppermute | solution.py:593
  19.4 0.0 copy-start
  19.4 1.2 pack_second.1
  20.6 0.0 collective-permute-done.3.own1
  20.7 0.6 collective-permute-start.4
  21.2 0.2 collective-permute-start.5
  21.5 1.5 %collective-permute-start.6 = (bf16[1040,128]{1,0:T(8,128)(2,1)S(1)}, bf16[1040,128]{1,0:T(8,128)(2,1)S(1)}, u32[]{:S(2)}, u32[]{:S(2)}) collective-permute-start(bf16[1040,128]{1,0:T(8,128)(2,1)S(1)} %get-tuple-element.69), channel_id=1, source_target_pairs={{0,3},{1,2},{2,1},{3,0},{4,7},{5,6},{6,5},{7,4},{8,11},{9,10},{10,... | collective-permute-start | bytes 798728 | tf_op jit(solution)/shard_map/ppermute | solution.py:588
  22.9 1.9 %collective-permute-start.8 = (bf16[1024,128]{1,0:T(8,128)(2,1)S(1)}, bf16[1024,128]{1,0:T(8,128)(2,1)S(1)}, u32[]{:S(2)}, u32[]{:S(2)}) collective-permute-start(bf16[1024,128]{1,0:T(8,128)(2,1)S(1)} %collective-permute-done.3.own1), channel_id=1, source_target_pairs={{0,4},{1,5},{2,6},{3,7},{4,8},{5,9},{6,10},{7,11},{8,12},{9,13},{1... | collective-permute-start | bytes 786440 | tf_op jit(solution)/shard_map/ppermute | solution.py:593
  24.9 0.0 collective-permute-done.4.a.s1
  24.9 4.3 %collective-permute-done.5.b.s2 = bf16[1040,128]{1,0:T(8,128)(2,1)S(1)} collective-permute-done((bf16[1040,128]{1,0:T(8,128)(2,1)S(1)}, bf16[1040,128]{1,0:T(8,128)(2,1)S(1)}, u32[]{:S(2)}, u32[]{:S(2)}) %collective-permute-start.5) | collective-permute-done | bytes 266272 | tf_op jit(solution)/shard_map/ppermute | solution.py:588
  29.2 5.9 %collective-permute-done.6.c.s3 = bf16[1040,128]{1,0:T(8,128)(2,1)S(1)} collective-permute-done((bf16[1040,128]{1,0:T(8,128)(2,1)S(1)}, bf16[1040,128]{1,0:T(8,128)(2,1)S(1)}, u32[]{:S(2)}, u32[]{:S(2)}) %collective-permute-start.6) | collective-permute-done | bytes 266272 | tf_op jit(solution)/shard_map/ppermute | solution.py:588
  35.1 0.6 maximum_convert_fusion.track_ref
  35.7 2.3 %plan.1 = (s32[8,24]{1,0:T(8,128)}, s32[8,2]{1,0:T(8,128)}) custom-call(s32[2]{0:T(128)} %copy-done.8, s32[8,16]{1,0:T(8,128)} %maximum_convert_fusion.track_ref), custom_call_target="tpu_custom_call" | custom-call | flops 1000000 | bytes 100000 | tf_op jit(solution)/shard_map/plan/pallas_call | solution.py:208
  38.0 0.0 copy-start.6
  38.0 0.0 copy-start.7
  38.1 0.0 collective-permute-done.7.rest1
  38.1 0.0 collective-permute-done.8.own2
  38.1 0.3 collective-permute-start.11
  38.4 0.3 copy-done.6
  38.7 0.0 copy-done.7
  38.7 11.8 %near0.1 = (f32[8,8,256]{2,1,0:T(8,128)S(1)}, f32[8,144,256]{2,1,0:T(8,128)S(1)}) custom-call(s32[8,24]{1,0:T(8,128)S(1)} %copy-done.6, s32[8,2]{1,0:T(8,128)S(1)} %copy-done.7, bf16[1024,128]{1,0:T(8,128)(2,1)S(1)} %get-tuple-element.65.own0, bf16[1536,128]{1,0:T(8,128)(2,1)S(1)} %stack.14.rest0, bf16[1024,128]{1,0:T(8,128)(2,1)S(1)} %collective-permute-done.3.own1, ...), custom_call_target="tpu_custom_call" | custom-call | flops 1000000 | bytes 100000 | tf_op jit(solution)/shard_map/near0/pallas_call | solution.py:335
  50.5 1.0 collective-permute-done.11.g2
  51.5 1.0 collective-permute-start.12
  52.5 0.1 collective-permute-start.13
  52.6 2.0 %collective-permute-start.9 = (bf16[1536,128]{1,0:T(8,128)(2,1)S(1)}, bf16[1536,128]{1,0:T(8,128)(2,1)S(1)}, u32[]{:S(2)}, u32[]{:S(2)}) collective-permute-start(bf16[1536,128]{1,0:T(8,128)(2,1)S(1)} %stack.15.rest0), channel_id=1, source_target_pairs={{0,4},{1,5},{2,6},{3,7},{4,8},{5,9},{6,10},{7,11},{8,12},{9,13},{1... | collective-permute-start | bytes 1179656 | tf_op jit(solution)/shard_map/ppermute | solution.py:593
  54.6 1.9 %collective-permute-start.14 = (bf16[1536,128]{1,0:T(8,128)(2,1)S(1)}, bf16[1536,128]{1,0:T(8,128)(2,1)S(1)}, u32[]{:S(2)}, u32[]{:S(2)}) collective-permute-start(bf16[1536,128]{1,0:T(8,128)(2,1)S(1)} %collective-permute-done.7.rest1), channel_id=1, source_target_pairs={{0,4},{1,5},{2,6},{3,7},{4,8},{5,9},{6,10},{7,11},{8,12},{9,13},{1... | collective-permute-start | bytes 1179656 | tf_op jit(solution)/shard_map/ppermute | solution.py:593
  56.6 8.0 %collective-permute-done.9.rest1 = bf16[1536,128]{1,0:T(8,128)(2,1)S(1)} collective-permute-done((bf16[1536,128]{1,0:T(8,128)(2,1)S(1)}, bf16[1536,128]{1,0:T(8,128)(2,1)S(1)}, u32[]{:S(2)}, u32[]{:S(2)}) %collective-permute-start.9) | collective-permute-done | bytes 393248 | tf_op jit(solution)/shard_map/ppermute | solution.py:593
  64.6 2.2 %collective-permute-start.10 = (bf16[1536,128]{1,0:T(8,128)(2,1)S(1)}, bf16[1536,128]{1,0:T(8,128)(2,1)S(1)}, u32[]{:S(2)}, u32[]{:S(2)}) collective-permute-start(bf16[1536,128]{1,0:T(8,128)(2,1)S(1)} %collective-permute-done.9.rest1), channel_id=1, source_target_pairs={{0,4},{1,5},{2,6},{3,7},{4,8},{5,9},{6,10},{7,11},{8,12},{9,13},{1... | collective-permute-start | bytes 1179656 | tf_op jit(solution)/shard_map/ppermute | solution.py:593
  66.8 11.9 %near1.1 = (f32[8,8,256]{2,1,0:T(8,128)S(1)}, f32[8,144,256]{2,1,0:T(8,128)S(1)}) custom-call(s32[8,24]{1,0:T(8,128)S(1)} %copy-done.6, s32[8,2]{1,0:T(8,128)S(1)} %copy-done.7, bf16[1024,128]{1,0:T(8,128)(2,1)S(1)} %get-tuple-element.65.own0, bf16[1536,128]{1,0:T(8,128)(2,1)S(1)} %stack.15.rest0, bf16[1024,128]{1,0:T(8,128)(2,1)S(1)} %collective-permute-done.3.own1, ...), custom_call_target="tpu_custom_call" | custom-call | flops 1000000 | bytes 100000 | tf_op jit(solution)/shard_map/near1/pallas_call | solution.py:335
  78.7 0.0 collective-permute-done.12.g1
  78.7 0.0 collective-permute-done.13.g3
  78.8 2.2 %grad_attn.1 = bf16[256,1024]{1,0:T(8,128)(2,1)S(1)} custom-call(s32[2]{0:T(128)S(1)} %copy-done.9, bf16[1024,1024]{1,0:T(8,128)(2,1)S(1)} %copy-done.1, bf16[256,1024]{1,0:T(8,128)(2,1)S(1)} %copy-done, bf16[256,1024]{1,0:T(8,128)(2,1)S(1)} %collective-permute-done.12.g1, bf16[256,1024]{1,0:T(8,128)(2,1)S(1)} %collective-permute-done.11.g2, ...), custom_call_target="tpu_custom_call" | custom-call | flops 1000000 | bytes 100000 | tf_op jit(solution)/shard_map/grad_attn/pallas_call | solution.py:166
  81.0 0.0 collective-permute-done.14.rest2
  81.0 2.8 %far0.1 = (bf16[128,1024]{1,0:T(8,128)(2,1)S(1)}, f32[8,8,256]{2,1,0:T(8,128)S(1)}, bf16[128,1024]{1,0:T(8,128)(2,1)S(1)}) custom-call(s32[2]{0:T(128)S(1)} %copy-done.9, s32[8,24]{1,0:T(8,128)S(1)} %copy-done.6, s32[8,2]{1,0:T(8,128)S(1)} %copy-done.7, bf16[1024,128]{1,0:T(8,128)(2,1)S(1)} %collective-permute-done.8.own2, ...), custom_call_target="tpu_custom_call" | custom-call | flops 1000000 | bytes 100000 | tf_op jit(solution)/shard_map/far0/pallas_call | solution.py:419
  83.8 10.9 %back0.1 = (bf16[768,128]{1,0:T(8,128)(2,1)S(1)}, bf16[768,128]{1,0:T(8,128)(2,1)S(1)}, bf16[768,128]{1,0:T(8,128)(2,1)S(1)}, bf16[768,128]{1,0:T(8,128)(2,1)S(1)}) custom-call(s32[8,24]{1,0:T(8,128)S(1)} %copy-done.6, s32[8,2]{1,0:T(8,128)S(1)} %copy-done.7, bf16[1024,128]{1,0:T(8,128)(2,1)S(1)} %get-tuple-element.65.own0, ...), custom_call_target="tpu_custom_call" | custom-call | flops 1000000 | bytes 100000 | tf_op jit(solution)/shard_map/back0/pallas_call | solution.py:536
  94.8 2.5 %collective-permute-start.15 = (bf16[768,128]{1,0:T(8,128)(2,1)S(1)}, bf16[768,128]{1,0:T(8,128)(2,1)S(1)}, u32[]{:S(2)}, u32[]{:S(2)}) collective-permute-start(bf16[768,128]{1,0:T(8,128)(2,1)S(1)} %get-tuple-element.92), channel_id=1, source_target_pairs={{0,1},{1,0},{2,3},{3,2},{4,5},{5,4},{6,7},{7,6},{8,9},{9,8},{10,11... | collective-permute-start | bytes 589832 | tf_op jit(solution)/shard_map/ppermute | solution.py:588
  97.3 0.2 collective-permute-start.16
  97.5 1.5 %collective-permute-start.17 = (bf16[768,128]{1,0:T(8,128)(2,1)S(1)}, bf16[768,128]{1,0:T(8,128)(2,1)S(1)}, u32[]{:S(2)}, u32[]{:S(2)}) collective-permute-start(bf16[768,128]{1,0:T(8,128)(2,1)S(1)} %get-tuple-element.94), channel_id=1, source_target_pairs={{0,3},{1,2},{2,1},{3,0},{4,7},{5,6},{6,5},{7,4},{8,11},{9,10},{10,... | collective-permute-start | bytes 589832 | tf_op jit(solution)/shard_map/ppermute | solution.py:588
  99.0 3.1 %far1.1 = (bf16[128,1024]{1,0:T(8,128)(2,1)S(1)}, f32[8,8,256]{2,1,0:T(8,128)S(1)}, bf16[64,1024]{1,0:T(8,128)(2,1)S(1)}, bf16[64,1024]{1,0:T(8,128)(2,1)S(1)}, ...) custom-call(s32[2]{0:T(128)S(1)} %copy-done.9, s32[8,24]{1,0:T(8,128)S(1)} %copy-done.6, s32[8,2]{1,0:T(8,128)S(1)} %copy-done.7, ...), custom_call_target="tpu_custom_call" | custom-call | flops 1000000 | bytes 100000 | tf_op jit(solution)/shard_map/far1/pallas_call | solution.py:419
  102.1 7.8 %collective-permute-start.21 = (bf16[64,1024]{1,0:T(8,128)(2,1)S(1)}, bf16[64,1024]{1,0:T(8,128)(2,1)S(1)}, u32[]{:S(2)}, u32[]{:S(2)}) collective-permute-start(bf16[64,1024]{1,0:T(8,128)(2,1)S(1)} %get-tuple-element.107), channel_id=1, source_target_pairs={{0,4},{1,5},{2,6},{3,7},{4,8},{5,9},{6,10},{7,11},{8,12},{9,13},{1... | collective-permute-start | bytes 393224 | tf_op jit(solution)/shard_map/ppermute | solution.py:652
  109.9 1.4 %collective-permute-start.22 = (bf16[64,1024]{1,0:T(8,128)(2,1)S(1)}, bf16[64,1024]{1,0:T(8,128)(2,1)S(1)}, u32[]{:S(2)}, u32[]{:S(2)}) collective-permute-start(bf16[64,1024]{1,0:T(8,128)(2,1)S(1)} %get-tuple-element.108), channel_id=1, source_target_pairs={{0,8},{1,9},{2,10},{3,11},{4,12},{5,13},{6,14},{7,15},{8,0},{9,1},... | collective-permute-start | bytes 393224 | tf_op jit(solution)/shard_map/ppermute | solution.py:652
  111.3 1.4 %collective-permute-start.23 = (bf16[64,1024]{1,0:T(8,128)(2,1)S(1)}, bf16[64,1024]{1,0:T(8,128)(2,1)S(1)}, u32[]{:S(2)}, u32[]{:S(2)}) collective-permute-start(bf16[64,1024]{1,0:T(8,128)(2,1)S(1)} %get-tuple-element.109), channel_id=1, source_target_pairs={{0,12},{1,13},{2,14},{3,15},{4,0},{5,1},{6,2},{7,3},{8,4},{9,5},{1... | collective-permute-start | bytes 393224 | tf_op jit(solution)/shard_map/ppermute | solution.py:652
  112.7 10.9 %back1.1 = (bf16[768,128]{1,0:T(8,128)(2,1)S(1)}, bf16[768,128]{1,0:T(8,128)(2,1)S(1)}, bf16[768,128]{1,0:T(8,128)(2,1)S(1)}, bf16[768,128]{1,0:T(8,128)(2,1)S(1)}) custom-call(s32[8,24]{1,0:T(8,128)S(1)} %copy-done.6, s32[8,2]{1,0:T(8,128)S(1)} %copy-done.7, bf16[1024,128]{1,0:T(8,128)(2,1)S(1)} %get-tuple-element.65.own0, ...), custom_call_target="tpu_custom_call" | custom-call | flops 1000000 | bytes 100000 | tf_op jit(solution)/shard_map/back1/pallas_call | solution.py:536
  123.6 1.1 collective-permute-start.18
  124.7 0.2 collective-permute-start.19
  124.9 0.0 collective-permute-done.21
  124.9 1.5 %collective-permute-start.20 = (bf16[768,128]{1,0:T(8,128)(2,1)S(1)}, bf16[768,128]{1,0:T(8,128)(2,1)S(1)}, u32[]{:S(2)}, u32[]{:S(2)}) collective-permute-start(bf16[768,128]{1,0:T(8,128)(2,1)S(1)} %get-tuple-element.102), channel_id=1, source_target_pairs={{0,3},{1,2},{2,1},{3,0},{4,7},{5,6},{6,5},{7,4},{8,11},{9,10},{10,... | collective-permute-start | bytes 589832 | tf_op jit(solution)/shard_map/ppermute | solution.py:588
  126.4 0.0 collective-permute-done.22
  126.4 0.0 collective-permute-done.23
  126.4 0.8 convert_add_fusion
  127.2 4.0 %collective-permute-done.19.refs_6_ = bf16[768,128]{1,0:T(8,128)(2,1)S(1)} collective-permute-done((bf16[768,128]{1,0:T(8,128)(2,1)S(1)}, bf16[768,128]{1,0:T(8,128)(2,1)S(1)}, u32[]{:S(2)}, u32[]{:S(2)}) %collective-permute-start.19) | collective-permute-done | bytes 196640 | tf_op jit(solution)/shard_map/ppermute | solution.py:588
  131.2 4.4 %collective-permute-done.20.refs_7_ = bf16[768,128]{1,0:T(8,128)(2,1)S(1)} collective-permute-done((bf16[768,128]{1,0:T(8,128)(2,1)S(1)}, bf16[768,128]{1,0:T(8,128)(2,1)S(1)}, u32[]{:S(2)}, u32[]{:S(2)}) %collective-permute-start.20) | collective-permute-done | bytes 196640 | tf_op jit(solution)/shard_map/ppermute | solution.py:588
  135.6 2.4 %unpack.1 = (bf16[256,1024]{1,0:T(8,128)(2,1)}, bf16[256,1024]{1,0:T(8,128)(2,1)}, bf16[256,1024]{1,0:T(8,128)(2,1)}) custom-call(s32[2]{0:T(128)S(1)} %copy-done.9, bf16[768,128]{1,0:T(8,128)(2,1)S(1)} %get-tuple-element.95.after.refs_0_, bf16[768,128]{1,0:T(8,128)(2,1)S(1)} %collective-permute-done.15.refs_1_, ...), custom_call_target="tpu_custom_call" | custom-call | flops 1000000 | bytes 100000 | tf_op jit(solution)/shard_map/unpack/pallas_call | solution.py:575
  (29 shorter events, 0.2 us)
Async XLA Ops:
  0.6 18.7 %copy-start.10 = (s32[2,16]{1,0:T(2,128)S(1)}, s32[2,16]{1,0:T(2,128)}, u32[]{:S(2)}) copy-start(s32[2,16]{1,0:T(2,128)} %param.9) | copy-start | bytes 388
  0.7 1.0 copy-start.2
  1.8 1.0 copy-start.4
  2.8 17.8 %copy-start.8 = (s32[2]{0:T(128)}, s32[2]{0:T(128)S(1)}, u32[]{:S(2)}) copy-start(s32[2]{0:T(128)S(1)} %pad_add_fusion.me_ref) | copy-start | bytes 28
  2.8 16.5 %copy-start.3 = (bf16[256,1024]{1,0:T(8,128)(2,1)S(1)}, bf16[256,1024]{1,0:T(8,128)(2,1)}, u32[]{:S(2)}) copy-start(bf16[256,1024]{1,0:T(8,128)(2,1)} %k_ref.3) | copy-start | bytes 1572868
  2.8 16.5 %copy-start.5 = (bf16[256,1024]{1,0:T(8,128)(2,1)S(1)}, bf16[256,1024]{1,0:T(8,128)(2,1)}, u32[]{:S(2)}) copy-start(bf16[256,1024]{1,0:T(8,128)(2,1)} %q_ref) | copy-start | bytes 1572868
  3.8 16.9 %collective-permute-start.3 = (bf16[1024,128]{1,0:T(8,128)(2,1)S(1)}, bf16[1024,128]{1,0:T(8,128)(2,1)S(1)}, u32[]{:S(2)}, u32[]{:S(2)}) collective-permute-start(bf16[1024,128]{1,0:T(8,128)(2,1)S(1)} %get-tuple-element.65.own0), channel_id=1, source_target_pairs={{0,4},{1,5},{2,6},{3,7},{4,8},{5,9},{6,10},{7,11},{8,12},{9,13},{1... | collective-permute-start | bytes 786440 | tf_op jit(solution)/shard_map/ppermute | solution.py:593
  7.0 2.7 %collective-permute-start = (bf16[512,128]{1,0:T(8,128)(2,1)S(1)}, bf16[512,128]{1,0:T(8,128)(2,1)S(1)}, u32[]{:S(2)}, u32[]{:S(2)}) collective-permute-start(bf16[512,128]{1,0:T(8,128)(2,1)S(1)} %get-tuple-element.57), channel_id=1, source_target_pairs={{0,1},{1,0},{2,3},{3,2},{4,5},{5,4},{6,7},{7,6},{8,9},{9,8},{10,11... | collective-permute-start | bytes 393224 | tf_op jit(solution)/shard_map/ppermute | solution.py:588
  8.0 5.1 %collective-permute-start.1 = (bf16[512,128]{1,0:T(8,128)(2,1)S(1)}, bf16[512,128]{1,0:T(8,128)(2,1)S(1)}, u32[]{:S(2)}, u32[]{:S(2)}) collective-permute-start(bf16[512,128]{1,0:T(8,128)(2,1)S(1)} %get-tuple-element.63), channel_id=1, source_target_pairs={{0,2},{1,3},{2,0},{3,1},{4,6},{5,7},{6,4},{7,5},{8,10},{9,11},{10,... | collective-permute-start | bytes 393224 | tf_op jit(solution)/shard_map/ppermute | solution.py:588
  8.3 7.8 %collective-permute-start.2 = (bf16[512,128]{1,0:T(8,128)(2,1)S(1)}, bf16[512,128]{1,0:T(8,128)(2,1)S(1)}, u32[]{:S(2)}, u32[]{:S(2)}) collective-permute-start(bf16[512,128]{1,0:T(8,128)(2,1)S(1)} %get-tuple-element.64), channel_id=1, source_target_pairs={{0,3},{1,2},{2,1},{3,0},{4,7},{5,6},{6,5},{7,4},{8,11},{9,10},{10,... | collective-permute-start | bytes 393224 | tf_op jit(solution)/shard_map/ppermute | solution.py:588
  16.1 21.9 %collective-permute-start.7 = (bf16[1536,128]{1,0:T(8,128)(2,1)S(1)}, bf16[1536,128]{1,0:T(8,128)(2,1)S(1)}, u32[]{:S(2)}, u32[]{:S(2)}) collective-permute-start(bf16[1536,128]{1,0:T(8,128)(2,1)S(1)} %stack.14.rest0), channel_id=1, source_target_pairs={{0,4},{1,5},{2,6},{3,7},{4,8},{5,9},{6,10},{7,11},{8,12},{9,13},{1... | collective-permute-start | bytes 1179656 | tf_op jit(solution)/shard_map/ppermute | solution.py:593
  19.4 18.7 %copy-start = (bf16[256,1024]{1,0:T(8,128)(2,1)S(1)}, bf16[256,1024]{1,0:T(8,128)(2,1)}, u32[]{:S(2)}) copy-start(bf16[256,1024]{1,0:T(8,128)(2,1)} %g0.5) | copy-start | bytes 1572868
  20.7 4.2 %collective-permute-start.4 = (bf16[1040,128]{1,0:T(8,128)(2,1)S(1)}, bf16[1040,128]{1,0:T(8,128)(2,1)S(1)}, u32[]{:S(2)}, u32[]{:S(2)}) collective-permute-start(bf16[1040,128]{1,0:T(8,128)(2,1)S(1)} %get-tuple-element.67), channel_id=1, source_target_pairs={{0,1},{1,0},{2,3},{3,2},{4,5},{5,4},{6,7},{7,6},{8,9},{9,8},{10,11... | collective-permute-start | bytes 798728 | tf_op jit(solution)/shard_map/ppermute | solution.py:588
  21.2 8.0 %collective-permute-start.5 = (bf16[1040,128]{1,0:T(8,128)(2,1)S(1)}, bf16[1040,128]{1,0:T(8,128)(2,1)S(1)}, u32[]{:S(2)}, u32[]{:S(2)}) collective-permute-start(bf16[1040,128]{1,0:T(8,128)(2,1)S(1)} %get-tuple-element.68), channel_id=1, source_target_pairs={{0,2},{1,3},{2,0},{3,1},{4,6},{5,7},{6,4},{7,5},{8,10},{9,11},{10,... | collective-permute-start | bytes 798728 | tf_op jit(solution)/shard_map/ppermute | solution.py:588
  21.5 13.6 %collective-permute-start.6 = (bf16[1040,128]{1,0:T(8,128)(2,1)S(1)}, bf16[1040,128]{1,0:T(8,128)(2,1)S(1)}, u32[]{:S(2)}, u32[]{:S(2)}) collective-permute-start(bf16[1040,128]{1,0:T(8,128)(2,1)S(1)} %get-tuple-element.69), channel_id=1, source_target_pairs={{0,3},{1,2},{2,1},{3,0},{4,7},{5,6},{6,5},{7,4},{8,11},{9,10},{10,... | collective-permute-start | bytes 798728 | tf_op jit(solution)/shard_map/ppermute | solution.py:588
  22.9 15.1 %collective-permute-start.8 = (bf16[1024,128]{1,0:T(8,128)(2,1)S(1)}, bf16[1024,128]{1,0:T(8,128)(2,1)S(1)}, u32[]{:S(2)}, u32[]{:S(2)}) collective-permute-start(bf16[1024,128]{1,0:T(8,128)(2,1)S(1)} %collective-permute-done.3.own1), channel_id=1, source_target_pairs={{0,4},{1,5},{2,6},{3,7},{4,8},{5,9},{6,10},{7,11},{8,12},{9,13},{1... | collective-permute-start | bytes 786440 | tf_op jit(solution)/shard_map/ppermute | solution.py:593
  38.0 0.7 copy-start.6
  38.0 0.7 copy-start.7
  38.1 13.4 %collective-permute-start.11 = (bf16[256,1024]{1,0:T(8,128)(2,1)S(1)}, bf16[256,1024]{1,0:T(8,128)(2,1)S(1)}, u32[]{:S(2)}, u32[]{:S(2)}) collective-permute-start(bf16[256,1024]{1,0:T(8,128)(2,1)S(1)} %copy-done), channel_id=1, source_target_pairs={{0,2},{1,3},{2,0},{3,1},{4,6},{5,7},{6,4},{7,5},{8,10},{9,11},{10,... | collective-permute-start | bytes 1572872 | tf_op jit(solution)/shard_map/ppermute | solution.py:588
  51.5 27.3 %copy-start.1 = (bf16[1024,1024]{1,0:T(8,128)(2,1)S(1)}, bf16[1024,1024]{1,0:T(8,128)(2,1)}, u32[]{:S(2)}) copy-start(bf16[1024,1024]{1,0:T(8,128)(2,1)} %w.1) | copy-start | bytes 6291460
  51.5 27.3 %copy-start.9 = (s32[2]{0:T(128)S(1)}, s32[2]{0:T(128)}, u32[]{:S(2)}) copy-start(s32[2]{0:T(128)} %copy-done.8) | copy-start | bytes 28
  51.5 27.2 %collective-permute-start.12 = (bf16[256,1024]{1,0:T(8,128)(2,1)S(1)}, bf16[256,1024]{1,0:T(8,128)(2,1)S(1)}, u32[]{:S(2)}, u32[]{:S(2)}) collective-permute-start(bf16[256,1024]{1,0:T(8,128)(2,1)S(1)} %copy-done), channel_id=1, source_target_pairs={{0,1},{1,0},{2,3},{3,2},{4,5},{5,4},{6,7},{7,6},{8,9},{9,8},{10,11... | collective-permute-start | bytes 1572872 | tf_op jit(solution)/shard_map/ppermute | solution.py:588
  52.5 26.2 %collective-permute-start.13 = (bf16[256,1024]{1,0:T(8,128)(2,1)S(1)}, bf16[256,1024]{1,0:T(8,128)(2,1)S(1)}, u32[]{:S(2)}, u32[]{:S(2)}) collective-permute-start(bf16[256,1024]{1,0:T(8,128)(2,1)S(1)} %collective-permute-done.11.g2), channel_id=1, source_target_pairs={{0,1},{1,0},{2,3},{3,2},{4,5},{5,4},{6,7},{7,6},{8,9},{9,8},{10,11... | collective-permute-start | bytes 1572872 | tf_op jit(solution)/shard_map/ppermute | solution.py:588
  52.6 12.0 %collective-permute-start.9 = (bf16[1536,128]{1,0:T(8,128)(2,1)S(1)}, bf16[1536,128]{1,0:T(8,128)(2,1)S(1)}, u32[]{:S(2)}, u32[]{:S(2)}) collective-permute-start(bf16[1536,128]{1,0:T(8,128)(2,1)S(1)} %stack.15.rest0), channel_id=1, source_target_pairs={{0,4},{1,5},{2,6},{3,7},{4,8},{5,9},{6,10},{7,11},{8,12},{9,13},{1... | collective-permute-start | bytes 1179656 | tf_op jit(solution)/shard_map/ppermute | solution.py:593
  54.6 26.3 %collective-permute-start.14 = (bf16[1536,128]{1,0:T(8,128)(2,1)S(1)}, bf16[1536,128]{1,0:T(8,128)(2,1)S(1)}, u32[]{:S(2)}, u32[]{:S(2)}) collective-permute-start(bf16[1536,128]{1,0:T(8,128)(2,1)S(1)} %collective-permute-done.7.rest1), channel_id=1, source_target_pairs={{0,4},{1,5},{2,6},{3,7},{4,8},{5,9},{6,10},{7,11},{8,12},{9,13},{1... | collective-permute-start | bytes 1179656 | tf_op jit(solution)/shard_map/ppermute | solution.py:593
  64.6 34.4 %collective-permute-start.10 = (bf16[1536,128]{1,0:T(8,128)(2,1)S(1)}, bf16[1536,128]{1,0:T(8,128)(2,1)S(1)}, u32[]{:S(2)}, u32[]{:S(2)}) collective-permute-start(bf16[1536,128]{1,0:T(8,128)(2,1)S(1)} %collective-permute-done.9.rest1), channel_id=1, source_target_pairs={{0,4},{1,5},{2,6},{3,7},{4,8},{5,9},{6,10},{7,11},{8,12},{9,13},{1... | collective-permute-start | bytes 1179656 | tf_op jit(solution)/shard_map/ppermute | solution.py:593
  94.8 16.5 %collective-permute-start.15 = (bf16[768,128]{1,0:T(8,128)(2,1)S(1)}, bf16[768,128]{1,0:T(8,128)(2,1)S(1)}, u32[]{:S(2)}, u32[]{:S(2)}) collective-permute-start(bf16[768,128]{1,0:T(8,128)(2,1)S(1)} %get-tuple-element.92), channel_id=1, source_target_pairs={{0,1},{1,0},{2,3},{3,2},{4,5},{5,4},{6,7},{7,6},{8,9},{9,8},{10,11... | collective-permute-start | bytes 589832 | tf_op jit(solution)/shard_map/ppermute | solution.py:588
  97.3 26.3 %collective-permute-start.16 = (bf16[768,128]{1,0:T(8,128)(2,1)S(1)}, bf16[768,128]{1,0:T(8,128)(2,1)S(1)}, u32[]{:S(2)}, u32[]{:S(2)}) collective-permute-start(bf16[768,128]{1,0:T(8,128)(2,1)S(1)} %get-tuple-element.93), channel_id=1, source_target_pairs={{0,2},{1,3},{2,0},{3,1},{4,6},{5,7},{6,4},{7,5},{8,10},{9,11},{10,... | collective-permute-start | bytes 589832 | tf_op jit(solution)/shard_map/ppermute | solution.py:588
  97.5 26.1 %collective-permute-start.17 = (bf16[768,128]{1,0:T(8,128)(2,1)S(1)}, bf16[768,128]{1,0:T(8,128)(2,1)S(1)}, u32[]{:S(2)}, u32[]{:S(2)}) collective-permute-start(bf16[768,128]{1,0:T(8,128)(2,1)S(1)} %get-tuple-element.94), channel_id=1, source_target_pairs={{0,3},{1,2},{2,1},{3,0},{4,7},{5,6},{6,5},{7,4},{8,11},{9,10},{10,... | collective-permute-start | bytes 589832 | tf_op jit(solution)/shard_map/ppermute | solution.py:588
  102.1 22.8 %collective-permute-start.21 = (bf16[64,1024]{1,0:T(8,128)(2,1)S(1)}, bf16[64,1024]{1,0:T(8,128)(2,1)S(1)}, u32[]{:S(2)}, u32[]{:S(2)}) collective-permute-start(bf16[64,1024]{1,0:T(8,128)(2,1)S(1)} %get-tuple-element.107), channel_id=1, source_target_pairs={{0,4},{1,5},{2,6},{3,7},{4,8},{5,9},{6,10},{7,11},{8,12},{9,13},{1... | collective-permute-start | bytes 393224 | tf_op jit(solution)/shard_map/ppermute | solution.py:652
  109.9 16.5 %collective-permute-start.22 = (bf16[64,1024]{1,0:T(8,128)(2,1)S(1)}, bf16[64,1024]{1,0:T(8,128)(2,1)S(1)}, u32[]{:S(2)}, u32[]{:S(2)}) collective-permute-start(bf16[64,1024]{1,0:T(8,128)(2,1)S(1)} %get-tuple-element.108), channel_id=1, source_target_pairs={{0,8},{1,9},{2,10},{3,11},{4,12},{5,13},{6,14},{7,15},{8,0},{9,1},... | collective-permute-start | bytes 393224 | tf_op jit(solution)/shard_map/ppermute | solution.py:652
  111.3 15.1 %collective-permute-start.23 = (bf16[64,1024]{1,0:T(8,128)(2,1)S(1)}, bf16[64,1024]{1,0:T(8,128)(2,1)S(1)}, u32[]{:S(2)}, u32[]{:S(2)}) collective-permute-start(bf16[64,1024]{1,0:T(8,128)(2,1)S(1)} %get-tuple-element.109), channel_id=1, source_target_pairs={{0,12},{1,13},{2,14},{3,15},{4,0},{5,1},{6,2},{7,3},{8,4},{9,5},{1... | collective-permute-start | bytes 393224 | tf_op jit(solution)/shard_map/ppermute | solution.py:652
  123.6 3.6 %collective-permute-start.18 = (bf16[768,128]{1,0:T(8,128)(2,1)S(1)}, bf16[768,128]{1,0:T(8,128)(2,1)S(1)}, u32[]{:S(2)}, u32[]{:S(2)}) collective-permute-start(bf16[768,128]{1,0:T(8,128)(2,1)S(1)} %get-tuple-element.100), channel_id=1, source_target_pairs={{0,1},{1,0},{2,3},{3,2},{4,5},{5,4},{6,7},{7,6},{8,9},{9,8},{10,11... | collective-permute-start | bytes 589832 | tf_op jit(solution)/shard_map/ppermute | solution.py:588
  124.7 6.5 %collective-permute-start.19 = (bf16[768,128]{1,0:T(8,128)(2,1)S(1)}, bf16[768,128]{1,0:T(8,128)(2,1)S(1)}, u32[]{:S(2)}, u32[]{:S(2)}) collective-permute-start(bf16[768,128]{1,0:T(8,128)(2,1)S(1)} %get-tuple-element.101), channel_id=1, source_target_pairs={{0,2},{1,3},{2,0},{3,1},{4,6},{5,7},{6,4},{7,5},{8,10},{9,11},{10,... | collective-permute-start | bytes 589832 | tf_op jit(solution)/shard_map/ppermute | solution.py:588
  124.9 10.6 %collective-permute-start.20 = (bf16[768,128]{1,0:T(8,128)(2,1)S(1)}, bf16[768,128]{1,0:T(8,128)(2,1)S(1)}, u32[]{:S(2)}, u32[]{:S(2)}) collective-permute-start(bf16[768,128]{1,0:T(8,128)(2,1)S(1)} %get-tuple-element.102), channel_id=1, source_target_pairs={{0,3},{1,2},{2,1},{3,0},{4,7},{5,6},{6,5},{7,4},{8,11},{9,10},{10,... | collective-permute-start | bytes 589832 | tf_op jit(solution)/shard_map/ppermute | solution.py:588
